TPU v7x, 512 devices: a whole 4x8x8 slice. The times are simulated.
512 devices in a mesh: grp: 32 (over y, z_hi, core), leaf: 16 (over z_lo, x).
Axes of the slice: x: 4, y: 8, z: 8 (z_hi: 2, z_lo: 4; z = z_hi * 4 + z_lo), core: 2. Of those that a mesh axis runs over, the one named last changes fastest.
Arguments:
- vectors: bfloat16 [32, 2097152], P(None, ('grp', 'leaf')), may hold values from -6 to 6
- offsets: bfloat16 [3, 2097152], P(None, ('grp', 'leaf')), may hold values from 0 to 1
- near_list: int32 [8192, 16], P(('grp', 'leaf')), may hold values from 0 to 8191, as said below
- near_count: int32 [8192], P(('grp', 'leaf')), may hold values from 8 to 16, as said below
- leaf_basis: bfloat16 [8192, 64, 256], P(('grp', 'leaf')), may hold values from -0.375 to 0.375
- far_list: int32 [8192, 16], P(('grp', 'leaf')), may hold values from 0 to 8191, as said below
- far_count: int32 [8192], P(('grp', 'leaf')), may hold values from 0 to 16, as said below
- leaf_coupling: bfloat16 [8192, 16, 64, 64], P(('grp', 'leaf')), as said below
- transfer: bfloat16 [8192, 64, 64], P(('grp', 'leaf')), may hold values from -0.75 to 0.75
- group_list: int32 [32, 16], P('grp'), may hold values from 0 to 31, as said below
- group_count: int32 [32], P('grp'), may hold values from 8 to 16, as said below
- group_coupling: bfloat16 [32, 16, 64, 64], P('grp', 'leaf'), may hold values from -0.01171875 to 0.01171875
Outputs:
- applied: bfloat16 [32, 2097152], P(None, ('grp', 'leaf'))
Inputs may be any that keep to these rules, and one draw needn't show every extreme that they name: `near_list`: the first near_count[l] entries of row l are distinct leaves of l's own group lying on l's device or on the devices just before and after it along leaf (16 consecutive leaves a device); the first entry is l itself and the remaining entries repeat l. `near_count`: the first leaf of every device has exactly 16. `far_list`: the first far_count[l] entries of row l are distinct leaves of l's own group other than l; the remaining entries repeat l. If leaf j stands in slot k < far_count[l] of row l, then l stands in some slot k2 < far_count[j] of row j. `far_count`: the first leaf of every group has exactly 16. If far_list[l, k] = j with k < far_count[l], and far_list[j, k2] = l with k2 < far_count[j], then leaf_coupling[j, k2] is the transpose of leaf_coupling[l, k]. `group_list`: the first group_count[g] entries of row g are distinct groups other than g; the remaining entries repeat g. `group_count`: group 0 has exactly 16.
All inputs are finite; a program needn't handle non-finite values.
Results may differ from a plain program's by a relative error of at most 0.005.
Values may be sent and summed in bfloat16 or wider, within the bound.
No kernel may reach another device: no remote copies, remote signals or barrier semaphores. Data moves between devices by JAX's collectives and lax.ppermute only.
A program may use at most 64 MiB of HBM per device.

v0:
```python
import jax
import jax.numpy as jnp
from jax import lax
from jax.sharding import PartitionSpec as P

inv_four_pi = 0.07957747154594767
soften = 0.01


def with_halo(shard, sides, width):
    for axis, dim in sides:
        count, length = (lax.axis_size(axis), shard.shape[dim])
        up = [(i, (i + 1) % count) for i in range(count - 1)]
        down = [(j, i) for i, j in up]
        last = lax.slice_in_dim(shard, length - width, length, axis=dim)
        first = lax.slice_in_dim(shard, 0, width, axis=dim)
        before = lax.ppermute(last, axis, up)
        after = lax.ppermute(first, axis, down)
        shard = jnp.concatenate([before, shard, after], axis=dim)
    return shard


def centres(leaf_ids):
    columns = []
    for axis_pos in range(3):
        summed = jnp.zeros_like(leaf_ids)
        for bit_pos in range(10):
            picked = jnp.bitwise_and(jnp.right_shift(leaf_ids, 3 * bit_pos + axis_pos), 1)
            summed = summed + jnp.left_shift(picked, bit_pos)
        columns.append(summed.astype(jnp.float32))
    return jnp.stack(columns)


def kernel_tile(source_pts, target_pts):
    squared = jnp.zeros(
        (source_pts.shape[0], source_pts.shape[2], target_pts.shape[1]), jnp.float32
    )
    for axis_pos in range(3):
        spacing = source_pts[:, axis_pos, :, None] - target_pts[axis_pos][None, None, :]
        squared = squared + spacing * spacing
    return inv_four_pi * lax.rsqrt(squared + soften)


def body(
    vectors,
    offsets,
    near_list,
    near_count,
    leaf_basis,
    far_list,
    far_count,
    leaf_coupling,
    transfer,
    group_list,
    group_count,
    group_coupling,
):
    leaf_devices = lax.axis_size("leaf")
    local_leaves = near_list.shape[0]
    near_slots = near_list.shape[1]
    far_slots = far_list.shape[1]
    vec_count = vectors.shape[0]
    leaf_width = vectors.shape[1] // local_leaves
    group_leaves = leaf_devices * local_leaves
    leaf_place = lax.axis_index("leaf")
    group_place = lax.axis_index("grp")
    device_first = (group_place * leaf_devices + leaf_place) * local_leaves
    group_first = group_place * group_leaves
    window_first = device_first - local_leaves
    stacked = jnp.concatenate([vectors, offsets], axis=0)
    widened = with_halo(stacked, (("leaf", 1),), local_leaves * leaf_width)
    window_vectors = widened[:vec_count].reshape(vec_count, 3 * local_leaves, leaf_width)
    window_ids = window_first + jnp.arange(3 * local_leaves, dtype=jnp.int32)
    window_pts = (
        widened[vec_count:].astype(jnp.float32).reshape(3, 3 * local_leaves, leaf_width)
        + centres(window_ids)[:, :, None]
    )
    slot_ids = jnp.arange(near_slots, dtype=jnp.int32)

    def near_step(running, target):
        sources = near_list[target] - window_first
        active_slots = slot_ids < near_count[target]
        source_pts = jnp.take(window_pts, sources, axis=1).transpose(1, 0, 2)
        target_pts = lax.dynamic_index_in_dim(window_pts, local_leaves + target, 1, keepdims=False)
        near_tile = jnp.where(
            active_slots[:, None, None], kernel_tile(source_pts, target_pts), 0.0
        ).astype(jnp.bfloat16)
        source_vectors = jnp.take(window_vectors, sources, axis=1)
        return (
            running,
            jnp.einsum(
                "vkb,kba->va", source_vectors, near_tile, preferred_element_type=jnp.float32
            ),
        )

    ignored, near_field = lax.scan(near_step, 0, jnp.arange(local_leaves, dtype=jnp.int32))
    leaf_vectors = vectors.reshape(vec_count, local_leaves, leaf_width)
    coeffs = jnp.einsum(
        "via,ira->ivr", leaf_vectors, leaf_basis, preferred_element_type=jnp.float32
    ).astype(jnp.bfloat16)
    far_active = jnp.arange(far_slots, dtype=jnp.int32)[None, :] < far_count[:, None]
    far_rows = far_list - group_first
    group_coeffs = lax.all_gather(coeffs, "leaf", axis=0, tiled=True)
    picked = jnp.take(group_coeffs, far_rows, axis=0)
    picked = jnp.where(far_active[:, :, None, None], picked, jnp.zeros((), jnp.bfloat16))
    far_field = jnp.einsum(
        "ikvs,ikrs->ivr", picked, leaf_coupling, preferred_element_type=jnp.float32
    )
    coarse_part = jnp.einsum("ivs,isr->vr", coeffs, transfer, preferred_element_type=jnp.float32)
    coarse = lax.psum(coarse_part, "leaf").astype(jnp.bfloat16)
    all_coarse = lax.all_gather(coarse[None], "grp", axis=0, tiled=True)
    group_active = jnp.arange(group_list.shape[1], dtype=jnp.int32) < group_count[0]
    own_slots = group_coupling.shape[1]
    slot_first = leaf_place * own_slots
    own_groups = lax.dynamic_slice_in_dim(group_list[0], slot_first, own_slots, 0)
    own_active = lax.dynamic_slice_in_dim(group_active, slot_first, own_slots, 0)
    picked_groups = jnp.where(
        own_active[:, None, None],
        jnp.take(all_coarse, own_groups, axis=0),
        jnp.zeros((), jnp.bfloat16),
    )
    coarse_term = jnp.einsum(
        "kvs,krs->vr", picked_groups, group_coupling[0], preferred_element_type=jnp.float32
    )
    coarse_out = lax.psum(coarse_term, "leaf")
    downward = jnp.einsum(
        "vs,irs->ivr", coarse_out.astype(jnp.bfloat16), transfer, preferred_element_type=jnp.float32
    )
    local_coeffs = (far_field + downward).astype(jnp.bfloat16)
    expanded = jnp.einsum(
        "ivr,ira->via", local_coeffs, leaf_basis, preferred_element_type=jnp.float32
    )
    result = jnp.transpose(near_field, (1, 0, 2)) + expanded
    return result.reshape(vec_count, local_leaves * leaf_width).astype(jnp.bfloat16)


def solution(mesh):
    placed = (
        P(None, ("grp", "leaf")),
        P(None, ("grp", "leaf")),
        P(("grp", "leaf"), None),
        P(("grp", "leaf")),
        P(("grp", "leaf"), None, None),
        P(("grp", "leaf"), None),
        P(("grp", "leaf")),
        P(("grp", "leaf"), None, None, None),
        P(("grp", "leaf"), None, None),
        P("grp", None),
        P("grp"),
        P("grp", "leaf", None, None),
    )
    return jax.shard_map(
        body, mesh=mesh, in_specs=placed, out_specs=P(None, ("grp", "leaf")), check_vma=False
    )
```

profile of v0, /device:TPU:8, one launch (start us, length us, event | category | flops | bytes accessed | tf_op | source)
XLA Modules:
  0.0 398.0 jit_solution(17522042291182980777)
XLA Ops:
  9.7 4.6 %collective-permute-start = (bf16[35,4096]{1,0:T(8,128)(2,1)S(1)}, bf16[35,4096]{1,0:T(8,128)(2,1)S(1)}, u32[]{:S(2)}, u32[]{:S(2)}) collective-permute-start(bf16[35,4096]{1,0:T(8,128)(2,1)S(1)} %constant_dynamic-update-slice_fusion), channel_id=1, source_target_pairs={{0,1},{1,2},{2,3},{3,4},{4,5},{5,6},{6,7},{7,8},{8,9},{9,10},{10,1... | collective-permute-start | bytes 860168 | tf_op jit(solution)/shard_map/ppermute | solution.py:17
  14.3 1.9 convolution_convert_fusion
  22.5 80.5 %psum.14 = bf16[32,64]{1,0:T(8,128)(2,1)S(1)} all-reduce(f32[32,64]{1,0:T(8,128)S(1)} %convolution_bitcast_fusion.1), channel_id=1, replica_groups=mesh['grp'=32,'leaf'=16] {'leaf'}, use_global_device_ids=true, to_apply=%region_2.3 | all-reduce | flops 2048 | bytes 12288 | tf_op jit(solution)/shard_map/psum | solution.py:110
  103.0 53.7 %all-gather = bf16[1024,64]{1,0:T(8,128)(2,1)S(1)} all-gather(bf16[32,64]{1,0:T(8,128)(2,1)S(1)} %psum.14), channel_id=2, replica_groups=mesh['grp'=32,'leaf'=16] {'grp'}, dimensions={0}, use_global_device_ids=true | all-gather | bytes 135168 | tf_op jit(solution)/shard_map/all_gather | solution.py:111
  156.7 1.5 fusion.30
  158.2 74.2 %psum.15 = bf16[32,64]{1,0:T(8,128)(2,1)S(1)} all-reduce(f32[32,64]{1,0:T(8,128)S(1)} %fusion.30), channel_id=1, replica_groups=mesh['grp'=32,'leaf'=16] {'leaf'}, use_global_device_ids=true, to_apply=%region_3.4 | all-reduce | flops 2048 | bytes 12288 | tf_op jit(solution)/shard_map/psum | solution.py:125
  233.6 148.9 %while.15 = (s32[]{:T(128)}, f32[16,32,256]{2,1,0:T(8,128)S(1)}, s32[16]{0:T(128)S(1)}, s32[16,16]{1,0:T(8,128)}, s32[]{:T(128)}, /*index=5*/bf16[32,48,256]{2,0...) while((s32[]{:T(128)}, f32[16,32,256]{2,1,0:T(8,128)S(1)}, ...), condition=%wide.region_1.2_spmd.clone, body=%wide.region_0.1_spmd.clone.sunk | while | flops 79836360 | bytes 1276693 | solution.py:96
  238.3 1.4 compare_and_fusion.3
  241.1 1.9 fusion.62
  247.7 1.4 compare_and_fusion.3
  250.4 1.9 fusion.62
  257.0 1.4 compare_and_fusion.3
  259.7 1.9 fusion.62
  266.3 1.4 compare_and_fusion.3
  269.0 1.9 fusion.62
  275.6 1.4 compare_and_fusion.3
  278.3 1.9 fusion.62
  284.9 1.4 compare_and_fusion.3
  287.6 1.9 fusion.62
  296.9 1.9 fusion.62
  306.2 1.9 fusion.62
  315.6 1.9 fusion.62
  324.9 1.9 fusion.62
  334.2 1.9 fusion.62
  343.5 1.9 fusion.62
  352.8 1.9 fusion.62
  362.1 1.9 fusion.62
  371.4 1.9 fusion.62
  380.7 1.9 fusion.62
  382.6 2.6 gather_fusion.2
  385.2 3.8 fusion.20
  389.0 1.4 fusion.23
  (236 shorter events, 75.6 us)
Async XLA Ops:
  6.5 7.7 %copy-start = (bf16[16,64,256]{2,1,0:T(8,128)(2,1)S(1)}, bf16[16,64,256]{2,1,0:T(8,128)(2,1)}, u32[]{:S(2)}) copy-start(bf16[16,64,256]{2,1,0:T(8,128)(2,1)} %param.18) | copy-start | bytes 1572868
  6.5 376.0 %all-gather.3.cloned.1.call-start = ((), (), s32[]{:S(2)}) async-start(), calls=%async_computation | async-start | bytes 2228224 | tf_op jit(solution)/shard_map/all_gather | solution.py:103
  8.4 224.9 %collective-permute-start.1 = (bf16[35,4096]{1,0:T(8,128)(2,1)S(1)}, bf16[35,4096]{1,0:T(8,128)(2,1)S(1)}, u32[]{:S(2)}, u32[]{:S(2)}) collective-permute-start(bf16[35,4096]{1,0:T(8,128)(2,1)S(1)} %constant_dynamic-update-slice_fusion), channel_id=1, source_target_pairs={{1,0},{2,1},{3,2},{4,3},{5,4},{6,5},{7,6},{8,7},{9,8},{10,9},{11,1... | collective-permute-start | bytes 860168 | tf_op jit(solution)/shard_map/ppermute | solution.py:18
  9.7 223.6 %collective-permute-start = (bf16[35,4096]{1,0:T(8,128)(2,1)S(1)}, bf16[35,4096]{1,0:T(8,128)(2,1)S(1)}, u32[]{:S(2)}, u32[]{:S(2)}) collective-permute-start(bf16[35,4096]{1,0:T(8,128)(2,1)S(1)} %constant_dynamic-update-slice_fusion), channel_id=1, source_target_pairs={{0,1},{1,2},{2,3},{3,4},{4,5},{5,6},{6,7},{7,8},{8,9},{9,10},{10,1... | collective-permute-start | bytes 860168 | tf_op jit(solution)/shard_map/ppermute | solution.py:17
  14.2 219.4 %copy-start.2 = (s32[16]{0:T(128)S(1)}, s32[16]{0:T(128)}, u32[]{:S(2)}) copy-start(s32[16]{0:T(128)} %param.17) | copy-start | bytes 196
  385.2 3.8 copy-start.1
Sparse Core Ops, SparseCore 0:
  16.3 92.5 all-gather.2
where the time goes:
time: 400 us; the launch traced here: 398 us
  blocking collectives  208 us (52%)
  local copies, waits for them, and re-layouts  47.7 us (12%)
  loops' own time  44.3 us (11%)
  matrix products  39.6 us (10%)
  other arithmetic  36.2 us (9%)
  between operations  15.9 us (4%)
  starting transfers between devices  5.86 us (1%)
    psum x1, blocking collectives, body(): coarse = lax.psum(coarse_part, 'leaf').astype(jnp.bfloat16)  80.5 us
    psum x1, blocking collectives, body(): coarse_out = lax.psum(coarse_term, 'leaf')  74.2 us
    all_gather x1, blocking collectives, body(): all_coarse = lax.all_gather(coarse[None], 'grp', axis=0, tiled=True)  53.7 us
    another operation x1, loops' own time, body(): lax.scan(near_step, 0, jnp.arange(local_leaves, dtype=jnp.int32))  44.3 us
    dot_general x16, matrix products, near_step(): jnp.einsum('vkb,kba->va', source_vectors, near_tile, preferred_element_ty...  29.8 us
    and x16, other arithmetic, near_step(): source_vectors = jnp.take(window_vectors, sources, axis=1)  21.9 us
    select_n x16, other arithmetic, near_step(): source_vectors = jnp.take(window_vectors, sources, axis=1)  11.1 us
    dynamic_slice x16, local copies, waits for them, and re-layouts, body(): lax.scan(near_step, 0, jnp.arange(local_leaves, dtype=jnp.int32))  10.5 us
  transfers between devices with their start and end apart: 3, of which 0 were waited for; matrix products, arithmetic and copies ran while one was open for 28% of the time, Pallas kernels for 0%

commit v1 on v0

v1 whole, which is shorter than its diff:
```python
import jax
import jax.numpy as jnp
from jax import lax
from jax.experimental import pallas as pl
from jax.experimental.pallas import tpu as pltpu
from jax.sharding import PartitionSpec as P

inv_four_pi = 0.07957747154594767
soften = 0.01
feature_depth = 128
slots_at_once = 4
id_bits = 5
vmem_bytes = 50 << 20

nt_dims = (((1,), (1,)), ((), ()))
nn_dims = (((1,), (0,)), ((), ()))
smem = pl.BlockSpec(memory_space=pltpu.SMEM)
vmem = pl.BlockSpec(memory_space=pltpu.VMEM)
params = pltpu.CompilerParams(vmem_limit_bytes=vmem_bytes)


def dot(left, right, dims):
    return lax.dot_general(left, right, dims, preferred_element_type=jnp.float32)


def pack(block):
    half = block.shape[0] // 2
    return jnp.concatenate([block[:half], block[half:]], axis=1)


def unpack(block):
    half = block.shape[1] // 2
    return jnp.concatenate([block[:, :half], block[:, half:]], axis=0)


def upward_kernel(vec_ref, off_ref, basis_ref, transfer_ref, group_ref, halo_ref, big_ref, small_ref):
    vecs, width = vec_ref.shape
    leaves = basis_ref.shape[0]
    points = width // leaves
    copies = big_ref.shape[0]
    rows = vecs // 2
    halo_ref[0:vecs, :] = vec_ref[...]
    halo_ref[vecs : vecs + off_ref.shape[0], :] = off_ref[...]
    part = jnp.zeros((vecs, transfer_ref.shape[2]), jnp.float32)
    for i in range(leaves):
        leaf = vec_ref[:, i * points : (i + 1) * points]
        coeff = dot(leaf, basis_ref[i], nt_dims).astype(jnp.bfloat16)
        part = part + dot(coeff, transfer_ref[i], nn_dims)
        packed = pack(coeff)
        for c in range(copies):
            big_ref[c, i * rows : (i + 1) * rows, :] = packed
    coupling = pack(group_ref[0, 0])
    packed_part = pack(part)
    for c in range(copies):
        big_ref[c, leaves * rows :, :] = coupling
        small_ref[c] = packed_part


def coarse_kernel(small_ref, out_ref):
    total = small_ref[0]
    for i in range(1, small_ref.shape[0]):
        total = total + small_ref[i]
    rounded = total.astype(jnp.bfloat16)
    for i in range(out_ref.shape[0]):
        out_ref[i] = rounded


def spread(ids, axis_pos):
    total = jnp.zeros_like(ids)
    for b in range(id_bits):
        bit = jnp.bitwise_and(jnp.right_shift(ids, 3 * b + axis_pos), 1)
        total = total + jnp.left_shift(bit, b)
    return total


def pieces(x):
    first = x.astype(jnp.bfloat16).astype(jnp.float32)
    second = (x - first).astype(jnp.bfloat16).astype(jnp.float32)
    return first, second, (x - first) - second


def near_kernel(list_ref, count_ref, own_ref, before_ref, after_ref, out_ref, source, target, vecs, wide):
    leaves, vec_count, width = out_ref.shape
    n = leaves * width
    base = list_ref[0, 0]
    rows = lax.broadcasted_iota(jnp.int32, (8, n), 0)
    lanes = lax.broadcasted_iota(jnp.int32, (8, n), 1)
    middle = spread(jnp.full((8, n), base, jnp.int32), rows) + jnp.where(rows == 0, 2, 1)
    vecs[3 * leaves] = jnp.zeros((vec_count, width), jnp.bfloat16)
    wide[...] = jnp.zeros((8, n), jnp.float32)
    for w, ref in enumerate((before_ref, own_ref, after_ref)):
        for i in range(leaves):
            vecs[w * leaves + i] = ref[0:vec_count, i * width : (i + 1) * width]
        wide[0:3, :] = ref[vec_count : vec_count + 3, :].astype(jnp.float32)
        o = wide[...]
        ids = base + (w - 1) * leaves + jnp.right_shift(lanes, 8)
        c = jnp.where(rows < 3, spread(ids, rows) - middle, 0).astype(jnp.float32)
        p = o + c
        norm = jnp.sum(p * p, axis=0, keepdims=True)
        n1, n2, n3 = pieces(norm)
        tail = jnp.where(rows < 6, 1.0, 0.0)
        tail = jnp.where(rows == 0, n1, jnp.where(rows == 1, n2, jnp.where(rows == 2, n3, tail)))
        blocks = [
            jnp.concatenate([o, o], axis=0).astype(jnp.bfloat16),
            jnp.concatenate([c, c], axis=0).astype(jnp.bfloat16),
            jnp.concatenate([tail, jnp.zeros_like(tail)], axis=0).astype(jnp.bfloat16),
        ]
        blank = jnp.zeros((feature_depth - 48, width), jnp.bfloat16)
        for i in range(leaves):
            span = slice(i * width, (i + 1) * width)
            for j, block in enumerate(blocks):
                source[w * leaves + i, 16 * j : 16 * (j + 1), :] = block[:, span]
            source[w * leaves + i, 48:, :] = blank
        if w == 1:
            t1, t2, t3 = pieces(norm + soften)
            tail = jnp.where(rows == 3, t1, jnp.where(rows == 4, t2, jnp.where(rows == 5, t3, 0.0)))
            tail = jnp.where(rows < 3, 1.0, tail)
            blank = jnp.zeros((feature_depth - 40, width), jnp.float32)
            for i in range(leaves):
                span = slice(i * width, (i + 1) * width)
                o_part, c_part = -2.0 * o[:, span], -2.0 * c[:, span]
                full = jnp.concatenate([o_part, c_part, o_part, c_part, tail[:, span], blank], axis=0)
                target[i] = jnp.transpose(full).astype(jnp.bfloat16)

    def one_leaf(t, carry):
        count = count_ref[t]
        points = target[t]

        def step(i, total):
            for g in range(slots_at_once):
                k = i * slots_at_once + g
                place = list_ref[t, k] - base + leaves
                squared = dot(points, source[place], nn_dims)
                tile = lax.rsqrt(squared).astype(jnp.bfloat16)
                total = total + dot(vecs[jnp.where(k < count, place, 3 * leaves)], tile, nt_dims)
            return total

        steps = (count + slots_at_once - 1) // slots_at_once
        total = lax.fori_loop(0, steps, step, jnp.zeros((vec_count, width), jnp.float32))
        out_ref[t] = total * inv_four_pi
        return carry

    lax.fori_loop(0, leaves, one_leaf, 0)


def far_kernel(list_ref, count_ref, big_ref, coupling_ref, out_ref):
    leaves, slots = coupling_ref.shape[:2]
    group_leaves = big_ref.shape[0] * leaves
    vec_count, rank = out_ref.shape[1:]
    rows = vec_count // 2

    def one_leaf(t, carry):
        count = count_ref[t]

        def step(i, total):
            for g in range(4):
                k = i * 4 + g
                j = lax.rem(list_ref[t, k], group_leaves)
                first = pl.multiple_of(lax.rem(j, leaves) * rows, rows)
                block = unpack(big_ref[lax.div(j, leaves), pl.ds(first, rows), :])
                block = jnp.where(k < count, block, jnp.zeros_like(block))
                total = total + dot(block, coupling_ref[t, k], nt_dims)
            return total

        out_ref[t] = lax.fori_loop(0, (count + 3) // 4, step, jnp.zeros((vec_count, rank), jnp.float32))
        return carry

    lax.fori_loop(0, leaves, one_leaf, 0)


def down_kernel(
    list_ref, count_ref, coarse_ref, big_ref, far_ref, near_ref, transfer_ref, basis_ref, out_ref
):
    leaves, vec_count, rank = far_ref.shape
    width = basis_ref.shape[2]
    coupling_row = leaves * (vec_count // 2)
    total = jnp.zeros((vec_count, rank), jnp.float32)
    for k in range(list_ref.shape[1]):
        block = unpack(coarse_ref[list_ref[0, k]])
        block = jnp.where(k < count_ref[0], block, jnp.zeros_like(block))
        total = total + dot(block, unpack(big_ref[k, coupling_row:, :]), nt_dims)
    coarse_out = total.astype(jnp.bfloat16)
    for i in range(leaves):
        local = far_ref[i] + dot(coarse_out, transfer_ref[i], nt_dims)
        result = near_ref[i] + dot(local.astype(jnp.bfloat16), basis_ref[i], nn_dims)
        out_ref[:, i * width : (i + 1) * width] = result.astype(jnp.bfloat16)


def cost(flops, moved, special=0):
    return pl.CostEstimate(flops=flops, bytes_accessed=moved, transcendentals=special)


def body(
    vectors,
    offsets,
    near_list,
    near_count,
    leaf_basis,
    far_list,
    far_count,
    leaf_coupling,
    transfer,
    group_list,
    group_count,
    group_coupling,
):
    members = lax.axis_size("leaf")
    groups = lax.axis_size("grp")
    vec_count, points = vectors.shape
    leaves, rank, width = leaf_basis.shape
    rows = vec_count // 2
    big_rows = leaves * rows + rank // 2
    stacked = vec_count + offsets.shape[0]
    up = [(i, i + 1) for i in range(members - 1)]
    down = [(j, i) for i, j in up]
    halo, big, small = pl.pallas_call(
        upward_kernel,
        out_shape=(
            jax.ShapeDtypeStruct((stacked, points), jnp.bfloat16),
            jax.ShapeDtypeStruct((members, big_rows, 2 * rank), jnp.bfloat16),
            jax.ShapeDtypeStruct((members, rows, 2 * rank), jnp.float32),
        ),
        in_specs=[vmem] * 5,
        out_specs=(vmem, vmem, vmem),
        compiler_params=params,
        cost_estimate=cost(40_000_000, 3_000_000),
        name="upward",
    )(vectors, offsets, leaf_basis, transfer, group_coupling)
    small_all = lax.all_to_all(small, "leaf", 0, 0, tiled=True)
    before = lax.ppermute(halo, "leaf", up)
    after = lax.ppermute(halo, "leaf", down)
    big_all = lax.all_to_all(big, "leaf", 0, 0, tiled=True)
    coarse = pl.pallas_call(
        coarse_kernel,
        out_shape=jax.ShapeDtypeStruct((groups, rows, 2 * rank), jnp.bfloat16),
        in_specs=[vmem],
        out_specs=vmem,
        compiler_params=params,
        cost_estimate=cost(40_000, 300_000),
        name="coarse",
    )(small_all)
    coarse_all = lax.all_to_all(coarse, "grp", 0, 0, tiled=True)
    near = pl.pallas_call(
        near_kernel,
        out_shape=jax.ShapeDtypeStruct((leaves, vec_count, width), jnp.float32),
        in_specs=[smem, smem, vmem, vmem, vmem],
        out_specs=vmem,
        scratch_shapes=[
            pltpu.VMEM((3 * leaves, feature_depth, width), jnp.bfloat16),
            pltpu.VMEM((leaves, width, feature_depth), jnp.bfloat16),
            pltpu.VMEM((3 * leaves + 1, vec_count, width), jnp.bfloat16),
            pltpu.VMEM((8, points), jnp.float32),
        ],
        compiler_params=params,
        cost_estimate=cost(16_000_000_000, 3_000_000, 15_000_000),
        name="near",
    )(near_list, near_count, halo, before, after)
    far = pl.pallas_call(
        far_kernel,
        out_shape=jax.ShapeDtypeStruct((leaves, vec_count, rank), jnp.float32),
        in_specs=[smem, smem, vmem, vmem],
        out_specs=vmem,
        compiler_params=params,
        cost_estimate=cost(1_000_000_000, 5_000_000),
        name="far",
    )(far_list, far_count, big_all, leaf_coupling)
    return pl.pallas_call(
        down_kernel,
        out_shape=jax.ShapeDtypeStruct((vec_count, points), jnp.bfloat16),
        in_specs=[smem, smem] + [vmem] * 6,
        out_specs=vmem,
        compiler_params=params,
        cost_estimate=cost(100_000_000, 3_000_000),
        name="downward",
    )(group_list, group_count, coarse_all, big_all, far, near, transfer, leaf_basis)


def solution(mesh):
    both = ("grp", "leaf")
    placed = (
        P(None, both),
        P(None, both),
        P(both, None),
        P(both),
        P(both, None, None),
        P(both, None),
        P(both),
        P(both, None, None, None),
        P(both, None, None),
        P("grp", None),
        P("grp"),
        P("grp", "leaf", None, None),
    )
    return jax.shard_map(body, mesh=mesh, in_specs=placed, out_specs=P(None, both), check_vma=False)
```

time: 400 us -> 119 us (0.30)
  the two profiles are of different devices: /device:TPU:8 before, /device:TPU:65 now
where the time goes in v1:
time: 119 us; the launch traced here: 118 us
  Pallas kernels  50.6 us (43%)
  starting transfers between devices  28.7 us (24%)
  waiting for transfers between devices  19.1 us (16%)
  blocking collectives  14.7 us (12%)
  local copies, waits for them, and re-layouts  4.45 us (4%)
    pallas_call x1, Pallas kernels, body(): pl.pallas_call(near_kernel, out_shape=jax.ShapeDtypeStruct((leaves, vec_c...  33.6 us
    all_to_all x1, waiting for transfers between devices, body(): big_all = lax.all_to_all(big, 'leaf', 0, 0, tiled=True)  19.1 us
    all_to_all x1, starting transfers between devices, body(): coarse_all = lax.all_to_all(coarse, 'grp', 0, 0, tiled=True)  15.8 us
    all_to_all x1, blocking collectives, body(): small_all = lax.all_to_all(small, 'leaf', 0, 0, tiled=True)  14.7 us
    pallas_call x1, Pallas kernels, body(): pl.pallas_call(far_kernel, out_shape=jax.ShapeDtypeStruct((leaves, vec_co...  10.7 us
    all_to_all x1, starting transfers between devices, body(): big_all = lax.all_to_all(big, 'leaf', 0, 0, tiled=True)  5.51 us
    unnamed x24, local copies, waits for them, and re-layouts  4.45 us
    ppermute x1, starting transfers between devices, body(): after = lax.ppermute(halo, 'leaf', down)  4.29 us
  transfers between devices with their start and end apart: 4, of which 1 were waited for; matrix products, arithmetic and copies ran while one was open for 0% of the time, Pallas kernels for 38%

profile of v1, /device:TPU:65, one launch (start us, length us, event | category | flops | bytes accessed | tf_op | source)
XLA Modules:
  0.0 118.3 jit_solution(2283888825216551958)
XLA Ops:
  0.0 1.0 copy-done
  1.0 0.0 copy-start.2
  1.0 0.9 copy-done.2
  2.0 0.9 copy-done.4
  2.9 0.8 copy-done.5
  3.7 0.7 copy-done.6
  4.4 1.8 %upward.1 = (bf16[35,4096]{1,0:T(8,128)(2,1)S(1)}, bf16[16,288,128]{2,1,0:T(8,128)(2,1)}, f32[16,16,128]{2,1,0:T(8,128)S(1)}) custom-call(bf16[32,4096]{1,0:T(8,128)(2,1)S(1)} %copy-done.4, bf16[3,4096]{1,0:T(4,128)(2,1)S(1)} %copy-done.5, bf16[16,64,256]{2,1,0:T(8,128)(2,1)S(1)} %copy-done, bf16[16,64,64]{2,1,0:T(8,128)(2,1)S(1)} %copy-done.2, ...), custom_call_target="tpu_custom_call" | custom-call | flops 40000000 | bytes 3000000 | tf_op jit(solution)/shard_map/upward/pallas_call | solution.py:216
  6.2 14.7 %all_to_all.15.small_ref = f32[16,16,128]{2,1,0:T(8,128)S(1)} all-to-all(f32[16,16,128]{2,1,0:T(8,128)S(1)} %get-tuple-element.8), channel_id=1, replica_groups=mesh['grp'=32,'leaf'=16] {'leaf'}, dimensions={0} | all-to-all | bytes 262144 | tf_op jit(solution)/shard_map/all_to_all | solution.py:229
  20.9 5.5 %all-to-all-start.2 = ((bf16[16,288,128]{2,1,0:T(8,128)(2,1)}), bf16[16,288,128]{2,1,0:T(8,128)(2,1)S(1)}, u32[]{:S(2)}, u32[]{:S(2)}) async-start(bf16[16,288,128]{2,1,0:T(8,128)(2,1)} %get-tuple-element.9), calls=%async_computation.2 | async-start | bytes 2359296 | tf_op jit(solution)/shard_map/all_to_all | solution.py:232
  26.4 3.1 %collective-permute-start = (bf16[35,4096]{1,0:T(8,128)(2,1)S(1)}, bf16[35,4096]{1,0:T(8,128)(2,1)S(1)}, u32[]{:S(2)}, u32[]{:S(2)}) collective-permute-start(bf16[35,4096]{1,0:T(8,128)(2,1)S(1)} %get-tuple-element.10.own_ref), channel_id=1, source_target_pairs={{0,1},{1,2},{2,3},{3,4},{4,5},{5,6},{6,7},{7,8},{8,9},{9,10},{10,1... | collective-permute-start | bytes 860168 | tf_op jit(solution)/shard_map/ppermute | solution.py:230
  29.5 4.3 %collective-permute-start.1 = (bf16[35,4096]{1,0:T(8,128)(2,1)S(1)}, bf16[35,4096]{1,0:T(8,128)(2,1)S(1)}, u32[]{:S(2)}, u32[]{:S(2)}) collective-permute-start(bf16[35,4096]{1,0:T(8,128)(2,1)S(1)} %get-tuple-element.10.own_ref), channel_id=1, source_target_pairs={{1,0},{2,1},{3,2},{4,3},{5,4},{6,5},{7,6},{8,7},{9,8},{10,9},{11,1... | collective-permute-start | bytes 860168 | tf_op jit(solution)/shard_map/ppermute | solution.py:231
  34.5 0.7 coarse.1
  35.1 19.1 %all-to-all-done.2.big_ref = bf16[16,288,128]{2,1,0:T(8,128)(2,1)S(1)} async-done(((bf16[16,288,128]{2,1,0:T(8,128)(2,1)}), bf16[16,288,128]{2,1,0:T(8,128)(2,1)S(1)}, u32[]{:S(2)}, u32[]{:S(2)}) %all-to-all-start.2) | async-done | bytes 1179680 | tf_op jit(solution)/shard_map/all_to_all | solution.py:232
  54.2 15.8 %all-to-all-start.1 = ((bf16[32,16,128]{2,1,0:T(8,128)(2,1)}), bf16[32,16,128]{2,1,0:T(8,128)(2,1)S(1)}, u32[]{:S(2)}, u32[]{:S(2)}) async-start(bf16[32,16,128]{2,1,0:T(8,128)(2,1)} %coarse.1), calls=%async_computation.1 | async-start | bytes 262144 | tf_op jit(solution)/shard_map/all_to_all | solution.py:242
  70.0 0.0 copy-start.7
  70.0 0.0 copy-start.8
  70.0 0.0 collective-permute-done.before_ref
  70.1 0.0 collective-permute-done.1.after_ref
  70.1 0.0 copy-done.10
  70.1 0.0 copy-done.11
  70.1 33.6 %near.1.near_ref = f32[16,32,256]{2,1,0:T(8,128)S(1)} custom-call(s32[16,16]{1,0:T(8,128)S(1)} %copy-done.10, s32[16]{0:T(128)S(1)} %copy-done.11, bf16[35,4096]{1,0:T(8,128)(2,1)S(1)} %get-tuple-element.10.own_ref, bf16[35,4096]{1,0:T(8,128)(2,1)S(1)} %collective-permute-done.before_ref, bf16[35,4096]{1,0:T(8,128)(2,1)S(1)} %collective-permute-done.1.after_ref), custom_call_target="tpu_custom_call" | custom-call | flops 16000000000 | bytes 3000000 | tf_op jit(solution)/shard_map/near/pallas_call | solution.py:243
  103.7 0.0 copy-done.7
  103.7 0.0 copy-done.8
  103.7 0.0 copy-start.1
  103.7 0.0 copy-start.3
  103.7 0.0 copy-start.9
  103.8 10.7 %far.1.far_ref = f32[16,32,64]{2,1,0:T(8,128)S(1)} custom-call(s32[16,16]{1,0:T(8,128)S(1)} %copy-done.7, s32[16]{0:T(128)S(1)} %copy-done.8, bf16[16,288,128]{2,1,0:T(8,128)(2,1)S(1)} %all-to-all-done.2.big_ref, bf16[16,16,64,64]{3,2,1,0:T(8,128)(2,1)} %coupling_ref.1), custom_call_target="tpu_custom_call" | custom-call | flops 1000000000 | bytes 5000000 | tf_op jit(solution)/shard_map/far/pallas_call | solution.py:258
  114.4 0.0 all-to-all-done.1.coarse_ref
  114.4 0.0 copy-done.1
  114.5 0.0 copy-done.3
  114.5 0.0 copy-done.9
  114.5 3.8 %downward.1 = bf16[32,4096]{1,0:T(8,128)(2,1)} custom-call(s32[1,16]{1,0:T(1,128)S(1)} %copy-done.9, s32[1]{0:T(128)S(6)} %copy.13.count_ref, bf16[32,16,128]{2,1,0:T(8,128)(2,1)S(1)} %all-to-all-done.1.coarse_ref, bf16[16,288,128]{2,1,0:T(8,128)(2,1)S(1)} %all-to-all-done.2.big_ref, f32[16,32,64]{2,1,0:T(8,128)S(1)} %far.1.far_ref, ...), custom_call_target="tpu_custom_call" | custom-call | flops 100000000 | bytes 3000000 | tf_op jit(solution)/shard_map/downward/pallas_call | solution.py:267
  (6 shorter events, 0.0 us)
Async XLA Ops:
  0.0 1.0 copy-start
  1.0 0.9 copy-start.2
  2.0 0.9 copy-start.4
  2.9 0.8 copy-start.5
  3.7 0.7 copy-start.6
  20.9 49.2 %copy-start.10 = (s32[16,16]{1,0:T(8,128)S(1)}, s32[16,16]{1,0:T(8,128)}, u32[]{:S(2)}) copy-start(s32[16,16]{1,0:T(8,128)} %list_ref.4) | copy-start | bytes 3076
  20.9 49.2 %copy-start.11 = (s32[16]{0:T(128)S(1)}, s32[16]{0:T(128)}, u32[]{:S(2)}) copy-start(s32[16]{0:T(128)} %count_ref.4) | copy-start | bytes 196
  20.9 33.3 %all-to-all-start.2 = ((bf16[16,288,128]{2,1,0:T(8,128)(2,1)}), bf16[16,288,128]{2,1,0:T(8,128)(2,1)S(1)}, u32[]{:S(2)}, u32[]{:S(2)}) async-start(bf16[16,288,128]{2,1,0:T(8,128)(2,1)} %get-tuple-element.9), calls=%async_computation.2 | async-start | bytes 2359296 | tf_op jit(solution)/shard_map/all_to_all | solution.py:232
  26.4 43.6 %collective-permute-start = (bf16[35,4096]{1,0:T(8,128)(2,1)S(1)}, bf16[35,4096]{1,0:T(8,128)(2,1)S(1)}, u32[]{:S(2)}, u32[]{:S(2)}) collective-permute-start(bf16[35,4096]{1,0:T(8,128)(2,1)S(1)} %get-tuple-element.10.own_ref), channel_id=1, source_target_pairs={{0,1},{1,2},{2,3},{3,4},{4,5},{5,6},{6,7},{7,8},{8,9},{9,10},{10,1... | collective-permute-start | bytes 860168 | tf_op jit(solution)/shard_map/ppermute | solution.py:230
  29.5 40.6 %collective-permute-start.1 = (bf16[35,4096]{1,0:T(8,128)(2,1)S(1)}, bf16[35,4096]{1,0:T(8,128)(2,1)S(1)}, u32[]{:S(2)}, u32[]{:S(2)}) collective-permute-start(bf16[35,4096]{1,0:T(8,128)(2,1)S(1)} %get-tuple-element.10.own_ref), channel_id=1, source_target_pairs={{1,0},{2,1},{3,2},{4,3},{5,4},{6,5},{7,6},{8,7},{9,8},{10,9},{11,1... | collective-permute-start | bytes 860168 | tf_op jit(solution)/shard_map/ppermute | solution.py:231
  54.2 60.2 %all-to-all-start.1 = ((bf16[32,16,128]{2,1,0:T(8,128)(2,1)}), bf16[32,16,128]{2,1,0:T(8,128)(2,1)S(1)}, u32[]{:S(2)}, u32[]{:S(2)}) async-start(bf16[32,16,128]{2,1,0:T(8,128)(2,1)} %coarse.1), calls=%async_computation.1 | async-start | bytes 262144 | tf_op jit(solution)/shard_map/all_to_all | solution.py:242
  70.0 33.7 %copy-start.7 = (s32[16,16]{1,0:T(8,128)S(1)}, s32[16,16]{1,0:T(8,128)}, u32[]{:S(2)}) copy-start(s32[16,16]{1,0:T(8,128)} %list_ref.3) | copy-start | bytes 3076
  70.0 33.7 %copy-start.8 = (s32[16]{0:T(128)S(1)}, s32[16]{0:T(128)}, u32[]{:S(2)}) copy-start(s32[16]{0:T(128)} %count_ref.3) | copy-start | bytes 196
  103.7 10.7 %copy-start.1 = (bf16[16,64,256]{2,1,0:T(8,128)(2,1)S(1)}, bf16[16,64,256]{2,1,0:T(8,128)(2,1)}, u32[]{:S(2)}) copy-start(bf16[16,64,256]{2,1,0:T(8,128)(2,1)} %basis_ref.3) | copy-start | bytes 1572868
  103.7 10.7 %copy-start.3 = (bf16[16,64,64]{2,1,0:T(8,128)(2,1)S(1)}, bf16[16,64,64]{2,1,0:T(8,128)(2,1)}, u32[]{:S(2)}) copy-start(bf16[16,64,64]{2,1,0:T(8,128)(2,1)} %transfer_ref.3) | copy-start | bytes 393220
  103.7 10.7 %copy-start.9 = (s32[1,16]{1,0:T(1,128)S(1)}, s32[1,16]{1,0:T(1,128)}, u32[]{:S(2)}) copy-start(s32[1,16]{1,0:T(1,128)} %list_ref.5) | copy-start | bytes 196

commit v2 on v1

v2 whole, which is shorter than its diff:
```python
import jax
import jax.numpy as jnp
from jax import lax
from jax.experimental import pallas as pl
from jax.experimental.pallas import tpu as pltpu
from jax.sharding import Mesh
from jax.sharding import PartitionSpec as P

inv_four_pi = 0.07957747154594767
soften = 0.01
sharpness = inv_four_pi**-2
feature_depth = 64
near_at_once = 4
far_at_once = 8
id_bits = 5
deep = 4
vmem_bytes = 50 << 20
whole_bytes = 63 << 20

nt_dims = (((1,), (1,)), ((), ()))
nn_dims = (((1,), (0,)), ((), ()))
smem = pl.BlockSpec(memory_space=pltpu.SMEM)
vmem = pl.BlockSpec(memory_space=pltpu.VMEM)
hbm = pl.BlockSpec(memory_space=pltpu.HBM)
params = pltpu.CompilerParams(vmem_limit_bytes=vmem_bytes)
whole = pltpu.CompilerParams(vmem_limit_bytes=whole_bytes)
anywhere = pl.BlockSpec(memory_space=pl.ANY)


def dot(left, right, dims):
    return lax.dot_general(left, right, dims, preferred_element_type=jnp.float32)


def pack(block):
    half = block.shape[0] // 2
    return jnp.concatenate([block[:half], block[half:]], axis=1)


def unpack(block):
    half = block.shape[1] // 2
    return jnp.concatenate([block[:, :half], block[:, half:]], axis=0)


def upward_kernel(
    vec_hbm, off_hbm, basis_hbm, transfer_hbm, group_hbm, halo_ref, big_ref, *scratch
):
    vec_ref, off_ref, basis_ref, transfer_ref, group_ref, sems = scratch
    sources = (vec_hbm, off_hbm, basis_hbm, transfer_hbm, group_hbm)
    copies_in = [
        pltpu.make_async_copy(src, dst, sems.at[i])
        for i, (src, dst) in enumerate(zip(sources, scratch[:5]))
    ]
    for copy in copies_in:
        copy.start()
    vecs, width = vec_ref.shape
    leaves = basis_ref.shape[0]
    points = width // leaves
    copies = big_ref.shape[0]
    rows = vecs // 2
    for copy in copies_in:
        copy.wait()
    halo_ref[0:vecs, :] = vec_ref[...]
    halo_ref[vecs : vecs + off_ref.shape[0], :] = off_ref[...]
    part = jnp.zeros((vecs, transfer_ref.shape[2]), jnp.float32)
    for i in range(leaves):
        leaf = vec_ref[:, i * points : (i + 1) * points]
        coeff = dot(leaf, basis_ref[i], nt_dims).astype(jnp.bfloat16)
        part = part + dot(coeff, transfer_ref[i], nn_dims)
        packed = pack(coeff)
        for c in range(copies):
            big_ref[c, i * rows : (i + 1) * rows, :] = packed
    coupling = pack(group_ref[0, 0])
    packed_part = pack(part)
    high = packed_part.astype(jnp.bfloat16)
    low = (packed_part - high.astype(jnp.float32)).astype(jnp.bfloat16)
    first = leaves * rows + coupling.shape[0]
    for c in range(copies):
        big_ref[c, leaves * rows : first, :] = coupling
        big_ref[c, first : first + rows, :] = high
        big_ref[c, first + rows :, :] = low


def regroup_kernel(big_ref, out_ref):
    deep, big_rows = big_ref.shape[:2]
    keep = (out_ref.shape[1] - big_rows) // (deep - 1)
    rows = (big_rows - keep) // 2
    total = jnp.zeros((rows, big_ref.shape[2]), jnp.float32)
    for i in range(deep):
        high = big_ref[i, keep : keep + rows, :].astype(jnp.float32)
        total = total + (high + big_ref[i, keep + rows :, :].astype(jnp.float32))
    high = total.astype(jnp.bfloat16)
    low = (total - high.astype(jnp.float32)).astype(jnp.bfloat16)
    for c in range(out_ref.shape[0]):
        for i in range(deep):
            out_ref[c, i * keep : (i + 1) * keep, :] = big_ref[i, :keep, :]
        out_ref[c, deep * keep : deep * keep + rows, :] = high
        out_ref[c, deep * keep + rows :, :] = low


def coarse_kernel(big_ref, near_ref, out_ref):
    members, big_rows = big_ref.shape[:2]
    rows = out_ref.shape[1]
    total = jnp.zeros(out_ref.shape[1:], jnp.float32)
    for i in range(members):
        high = big_ref[i, big_rows - 2 * rows : big_rows - rows, :].astype(jnp.float32)
        total = total + (high + big_ref[i, big_rows - rows :, :].astype(jnp.float32))
    rounded = total.astype(jnp.bfloat16)
    for i in range(out_ref.shape[0]):
        out_ref[i] = rounded


def spread(ids, axis_pos):
    total = jnp.zeros_like(ids)
    for b in range(id_bits):
        bit = jnp.bitwise_and(jnp.right_shift(ids, 3 * b + axis_pos), 1)
        total = total + jnp.left_shift(bit, b)
    return total


def pieces(x):
    first = x.astype(jnp.bfloat16).astype(jnp.float32)
    second = (x - first).astype(jnp.bfloat16).astype(jnp.float32)
    return first, second, (x - first) - second


def list_pairs(count_ref, leaves, chunk, put, pad):
    def one_leaf(t, place):
        return lax.fori_loop(0, count_ref[t], lambda k, q: put(t, k, q), place)

    total = lax.fori_loop(0, leaves, one_leaf, 0)
    chunks = (total + chunk - 1) // chunk

    def fill(q, carry):
        pad(q)
        return carry

    lax.fori_loop(total, chunks * chunk + chunk, fill, 0)
    return chunks


def near_kernel(
    list_ref, count_ref, own_ref, before_ref, after_ref, first_ref, out_ref, *scratch
):
    source, target, vecs, wide, to_leaf, from_leaf, tiles_a, tiles_b = scratch
    leaves = out_ref.shape[0] - 1
    vec_count, width = out_ref.shape[1:]
    n = leaves * width
    base = list_ref[0, 0]
    rows = lax.broadcasted_iota(jnp.int32, (8, n), 0)
    lanes = lax.broadcasted_iota(jnp.int32, (8, n), 1)
    middle = spread(jnp.full((8, n), base, jnp.int32), rows) + jnp.where(rows == 0, 2, 1)
    wide[...] = jnp.zeros((8, n), jnp.float32)
    blank = jnp.zeros((128 - 56, width), jnp.float32)
    for w, ref in enumerate((before_ref, own_ref, after_ref)):
        for i in range(leaves):
            vecs[w * leaves + i] = ref[0:vec_count, i * width : (i + 1) * width]
        wide[0:3, :] = ref[vec_count : vec_count + 3, :].astype(jnp.float32)
        o = wide[...]
        ids = base + (w - 1) * leaves + jnp.right_shift(lanes, 8)
        c = jnp.where(rows < 3, spread(ids, rows) - middle, 0).astype(jnp.float32)
        p = o + c
        norm = jnp.sum(p * p, axis=0, keepdims=True)
        n1, n2, n3 = pieces(norm * sharpness)
        tail = jnp.where(rows < 6, 1.0, 0.0)
        tail = jnp.where(rows == 0, n1, jnp.where(rows == 1, n2, jnp.where(rows == 2, n3, tail)))
        for i in range(leaves):
            span = slice(i * width, (i + 1) * width)
            o_part, c_part = o[:, span], c[:, span]
            full = jnp.concatenate([o_part] * 3 + [c_part] * 3 + [tail[:, span], blank], axis=0)
            source[w * leaves + i] = jnp.transpose(full).astype(jnp.bfloat16)
        if w == 1:
            t1, t2, t3 = pieces((norm + soften) * sharpness)
            p1, p2, p3 = pieces(p * (-2.0 * sharpness))
            tail = jnp.where(rows == 3, t1, jnp.where(rows == 4, t2, jnp.where(rows == 5, t3, 0.0)))
            tail = jnp.where(rows < 3, 1.0, tail)
            halves = [(p1, p2), (p3, p1), (p2, p3), (tail, jnp.zeros_like(tail))]
            for j, pair in enumerate(halves):
                block = jnp.concatenate(pair, axis=0).astype(jnp.bfloat16)
                for i in range(leaves):
                    target[i, 16 * j : 16 * (j + 1), :] = block[:, i * width : (i + 1) * width]

    def put(t, k, q):
        to_leaf[q] = t
        from_leaf[q] = list_ref[t, k] - base + leaves
        return q + 1

    def pad(q):
        to_leaf[q] = leaves
        from_leaf[q] = 0

    pairs = list_pairs(count_ref, leaves, 2 * near_at_once, put, pad)
    out_ref[...] = jnp.zeros_like(out_ref)

    def make_tiles(first, tiles):
        for g in range(near_at_once):
            t = jnp.minimum(to_leaf[first + g], leaves - 1)
            points = source[from_leaf[first + g]][:, :feature_depth]
            tiles[g] = lax.rsqrt(dot(points, target[t], nn_dims)).astype(jnp.bfloat16)

    def use_tiles(first, tiles):
        for g in range(near_at_once):
            out_ref[to_leaf[first + g]] += dot(vecs[from_leaf[first + g]], tiles[g], nn_dims)

    make_tiles(0, tiles_a)

    def step(i, carry):
        first = 2 * near_at_once * i
        make_tiles(first + near_at_once, tiles_b)
        use_tiles(first, tiles_a)
        make_tiles(first + 2 * near_at_once, tiles_a)
        use_tiles(first + near_at_once, tiles_b)
        return carry

    lax.fori_loop(0, pairs, step, 0)


def far_kernel(list_ref, count_ref, big_ref, coupling_ref, out_ref, to_leaf, slot, from_leaf):
    leaves, slots = coupling_ref.shape[:2]
    across = big_ref.shape[0]
    rows = out_ref.shape[1] // 2
    keep = leaves * rows + coupling_ref.shape[2] // 2
    group_leaves = across * deep * leaves

    def put(t, k, q):
        to_leaf[q] = t
        slot[q] = k
        from_leaf[q] = lax.rem(list_ref[t, k], group_leaves)
        return q + 1

    def pad(q):
        to_leaf[q] = leaves
        slot[q] = 0
        from_leaf[q] = 0

    chunks = list_pairs(count_ref, leaves, far_at_once, put, pad)
    out_ref[...] = jnp.zeros_like(out_ref)

    def step(i, carry):
        terms = []
        for g in range(far_at_once):
            q = i * far_at_once + g
            j = from_leaf[q]
            holder = lax.div(j, leaves)
            first = lax.div(holder, across) * keep + lax.rem(j, leaves) * rows
            first = pl.multiple_of(first, rows)
            block = unpack(big_ref[lax.rem(holder, across), pl.ds(first, rows), :])
            coupling = coupling_ref[jnp.minimum(to_leaf[q], leaves - 1), slot[q]]
            terms.append(dot(block, coupling, nt_dims))
        for g, term in enumerate(terms):
            out_ref[to_leaf[i * far_at_once + g]] += term
        return carry

    lax.fori_loop(0, chunks, step, 0)


def down_kernel(
    list_ref, count_ref, coarse_ref, big_ref, far_ref, near_ref, transfer_ref, basis_ref, out_ref
):
    leaves, rank, width = basis_ref.shape
    vec_count = out_ref.shape[0]
    across = big_ref.shape[0]
    keep = leaves * (vec_count // 2) + rank // 2
    total = jnp.zeros((vec_count, rank), jnp.float32)
    for k in range(list_ref.shape[1]):
        block = unpack(coarse_ref[list_ref[0, k]])
        block = jnp.where(k < count_ref[0], block, jnp.zeros_like(block))
        last = (k // across + 1) * keep
        coupling = unpack(big_ref[k % across, last - rank // 2 : last, :])
        total = total + dot(block, coupling, nt_dims)
    coarse_out = total.astype(jnp.bfloat16)
    for i in range(leaves):
        local = far_ref[i] + dot(coarse_out, transfer_ref[i], nt_dims)
        result = near_ref[i] + dot(local.astype(jnp.bfloat16), basis_ref[i], nn_dims)
        out_ref[:, i * width : (i + 1) * width] = result.astype(jnp.bfloat16)


def cost(flops, moved, special=0):
    return pl.CostEstimate(flops=flops, bytes_accessed=moved, transcendentals=special)


def body(
    vectors,
    offsets,
    near_list,
    near_count,
    leaf_basis,
    far_list,
    far_count,
    leaf_coupling,
    transfer,
    group_list,
    group_count,
    group_coupling,
):
    across = lax.axis_size("across")
    members = lax.axis_size("deep") * across
    groups = lax.axis_size("grp")
    vec_count, points = vectors.shape
    leaves, rank, width = leaf_basis.shape
    rows = vec_count // 2
    keep = leaves * rows + rank // 2
    stacked = vec_count + offsets.shape[0]
    up = [(i, i + 1) for i in range(members - 1)]
    down = [(j, i) for i, j in up]
    inputs = (vectors, offsets, leaf_basis, transfer, group_coupling)
    halo, big = pl.pallas_call(
        upward_kernel,
        out_shape=(
            jax.ShapeDtypeStruct((stacked, points), jnp.bfloat16),
            jax.ShapeDtypeStruct((deep, keep + 2 * rows, 2 * rank), jnp.bfloat16),
        ),
        in_specs=[hbm] * 5,
        out_specs=(vmem, vmem),
        scratch_shapes=[pltpu.VMEM(x.shape, x.dtype) for x in inputs]
        + [pltpu.SemaphoreType.DMA((len(inputs),))],
        compiler_params=whole,
        cost_estimate=cost(40_000_000, 3_000_000),
        name="upward",
    )(*inputs)
    deep_all = lax.all_to_all(big, "deep", 0, 0, tiled=True)
    before = lax.ppermute(halo, ("deep", "across"), up)
    after = lax.ppermute(halo, ("deep", "across"), down)
    wide = pl.pallas_call(
        regroup_kernel,
        out_shape=jax.ShapeDtypeStruct((across, deep * keep + 2 * rows, 2 * rank), jnp.bfloat16),
        in_specs=[vmem],
        out_specs=vmem,
        compiler_params=params,
        cost_estimate=cost(40_000, 2_000_000),
        name="regroup",
    )(deep_all)
    big_all = lax.all_to_all(wide, "across", 0, 0, tiled=True)
    near_pairs = near_list.size + 4 * near_at_once
    far_pairs = far_list.size + 2 * far_at_once
    near = pl.pallas_call(
        near_kernel,
        out_shape=jax.ShapeDtypeStruct((leaves + 1, vec_count, width), jnp.float32),
        in_specs=[smem, smem, vmem, vmem, vmem, anywhere],
        out_specs=vmem,
        scratch_shapes=[
            pltpu.VMEM((3 * leaves, width, 128), jnp.bfloat16),
            pltpu.VMEM((leaves, feature_depth, width), jnp.bfloat16),
            pltpu.VMEM((3 * leaves, vec_count, width), jnp.bfloat16),
            pltpu.VMEM((8, points), jnp.float32),
            pltpu.SMEM((near_pairs,), jnp.int32),
            pltpu.SMEM((near_pairs,), jnp.int32),
            pltpu.VMEM((near_at_once, width, width), jnp.bfloat16),
            pltpu.VMEM((near_at_once, width, width), jnp.bfloat16),
        ],
        compiler_params=params,
        cost_estimate=cost(16_000_000_000, 3_000_000, 15_000_000),
        name="near",
    )(near_list, near_count, halo, before, after, wide)
    coarse = pl.pallas_call(
        coarse_kernel,
        out_shape=jax.ShapeDtypeStruct((groups, rows, 2 * rank), jnp.bfloat16),
        in_specs=[vmem, anywhere],
        out_specs=vmem,
        compiler_params=params,
        cost_estimate=cost(40_000, 300_000),
        name="coarse",
    )(big_all, near)
    coarse_all = lax.all_to_all(coarse, "grp", 0, 0, tiled=True)
    far = pl.pallas_call(
        far_kernel,
        out_shape=jax.ShapeDtypeStruct((leaves + 1, vec_count, rank), jnp.float32),
        in_specs=[smem, smem, vmem, vmem],
        out_specs=vmem,
        scratch_shapes=[pltpu.SMEM((far_pairs,), jnp.int32) for _ in range(3)],
        compiler_params=params,
        cost_estimate=cost(1_000_000_000, 5_000_000),
        name="far",
    )(far_list, far_count, big_all, leaf_coupling)
    return pl.pallas_call(
        down_kernel,
        out_shape=jax.ShapeDtypeStruct((vec_count, points), jnp.bfloat16),
        in_specs=[smem, smem] + [vmem] * 6,
        out_specs=vmem,
        compiler_params=params,
        cost_estimate=cost(100_000_000, 3_000_000),
        name="downward",
    )(group_list, group_count, coarse_all, big_all, far, near, transfer, leaf_basis)


def solution(mesh):
    groups, members = mesh.devices.shape
    split = Mesh(mesh.devices.reshape(groups, deep, members // deep), ("grp", "deep", "across"))
    leaf = ("deep", "across")
    both = ("grp",) + leaf
    placed = (
        P(None, both),
        P(None, both),
        P(both, None),
        P(both),
        P(both, None, None),
        P(both, None),
        P(both),
        P(both, None, None, None),
        P(both, None, None),
        P("grp", None),
        P("grp"),
        P("grp", leaf, None, None),
    )
    return jax.shard_map(body, mesh=split, in_specs=placed, out_specs=P(None, both), check_vma=False)
```

time: 119 us -> 76.5 us (0.64)
  the two profiles are of different devices: /device:TPU:65 before, /device:TPU:7 now
where the time goes in v2:
time: 76.5 us; the launch traced here: 76.2 us
  starting transfers between devices  34 us (44%)
  Pallas kernels  33.4 us (44%)
  waiting for transfers between devices  7.95 us (10%)
  between operations  0.77 us (1%)
    all_to_all x1, starting transfers between devices, body(): coarse_all = lax.all_to_all(coarse, 'grp', 0, 0, tiled=True)  17.4 us
    pallas_call x1, Pallas kernels, body(): pl.pallas_call(near_kernel, out_shape=jax.ShapeDtypeStruct((leaves + 1, v...  16.6 us
    pallas_call x1, Pallas kernels, body(): pl.pallas_call(far_kernel, out_shape=jax.ShapeDtypeStruct((leaves + 1, ve...  8.21 us
    all_to_all x1, starting transfers between devices, body(): deep_all = lax.all_to_all(big, 'deep', 0, 0, tiled=True)  6.99 us
    all_to_all x1, starting transfers between devices, body(): big_all = lax.all_to_all(wide, 'across', 0, 0, tiled=True)  4.34 us
    all_to_all x1, waiting for transfers between devices, body(): coarse_all = lax.all_to_all(coarse, 'grp', 0, 0, tiled=True)  4.26 us
    pallas_call x1, Pallas kernels, body(): pl.pallas_call(down_kernel, out_shape=jax.ShapeDtypeStruct((vec_count, po...  3.82 us
    all_to_all x1, waiting for transfers between devices, body(): deep_all = lax.all_to_all(big, 'deep', 0, 0, tiled=True)  3.37 us
  transfers between devices with their start and end apart: 5, of which 3 were waited for; matrix products, arithmetic and copies ran while one was open for 0% of the time, Pallas kernels for 34%

profile of v2, /device:TPU:7, one launch (start us, length us, event | category | flops | bytes accessed | tf_op | source)
XLA Modules:
  0.0 76.2 jit_solution(8855826291787434906)
XLA Ops:
  0.0 2.9 %upward.1 = (bf16[35,4096]{1,0:T(8,128)(2,1)}, bf16[4,320,128]{2,1,0:T(8,128)(2,1)}) custom-call(bf16[32,4096]{1,0:T(8,128)(2,1)} %vec_hbm.1, bf16[3,4096]{1,0:T(4,128)(2,1)} %off_hbm.1, bf16[16,64,256]{2,1,0:T(8,128)(2,1)} %basis_ref.1, bf16[16,64,64]{2,1,0:T(8,128)(2,1)} %transfer_ref.1, bf16[1,1,64,64]{3,2,1,0:T(8,128)(2,1)} %group_hbm.1), custom_call_target="tpu_custom_call" | custom-call | flops 40000000 | bytes 3000000 | tf_op jit(solution)/shard_map/upward/pallas_call | solution.py:306
  2.9 7.0 %all-to-all-start = ((bf16[4,320,128]{2,1,0:T(8,128)(2,1)}), bf16[4,320,128]{2,1,0:T(8,128)(2,1)S(1)}, u32[]{:S(2)}, u32[]{:S(2)}) async-start(bf16[4,320,128]{2,1,0:T(8,128)(2,1)} %get-tuple-element.7), calls=%async_computation | async-start | bytes 655360 | tf_op jit(solution)/shard_map/all_to_all | solution.py:320
  9.9 3.3 %collective-permute-start = (bf16[35,4096]{1,0:T(8,128)(2,1)}, bf16[35,4096]{1,0:T(8,128)(2,1)S(1)}, u32[]{:S(2)}, u32[]{:S(2)}) collective-permute-start(bf16[35,4096]{1,0:T(8,128)(2,1)} %get-tuple-element.8.own_ref), channel_id=1, source_target_pairs={{0,1},{1,2},{2,3},{3,4},{4,5},{5,6},{6,7},{7,8},{8,9},{9,10},{10,1... | collective-permute-start | bytes 860168 | tf_op jit(solution)/shard_map/ppermute | solution.py:321
  13.2 2.0 %collective-permute-start.1 = (bf16[35,4096]{1,0:T(8,128)(2,1)}, bf16[35,4096]{1,0:T(8,128)(2,1)S(1)}, u32[]{:S(2)}, u32[]{:S(2)}) collective-permute-start(bf16[35,4096]{1,0:T(8,128)(2,1)} %get-tuple-element.8.own_ref), channel_id=1, source_target_pairs={{1,0},{2,1},{3,2},{4,3},{5,4},{6,5},{7,6},{8,7},{9,8},{10,9},{11,1... | collective-permute-start | bytes 860168 | tf_op jit(solution)/shard_map/ppermute | solution.py:322
  15.2 3.4 %all-to-all-done.big_ref = bf16[4,320,128]{2,1,0:T(8,128)(2,1)S(1)} async-done(((bf16[4,320,128]{2,1,0:T(8,128)(2,1)}), bf16[4,320,128]{2,1,0:T(8,128)(2,1)S(1)}, u32[]{:S(2)}, u32[]{:S(2)}) %all-to-all-start) | async-done | bytes 327712 | tf_op jit(solution)/shard_map/all_to_all | solution.py:320
  18.5 1.2 %regroup.1.first_ref = bf16[4,1184,128]{2,1,0:T(8,128)(2,1)} custom-call(bf16[4,320,128]{2,1,0:T(8,128)(2,1)S(1)} %all-to-all-done.big_ref), custom_call_target="tpu_custom_call" | custom-call | flops 40000 | bytes 2000000 | tf_op jit(solution)/shard_map/regroup/pallas_call | solution.py:323
  19.8 0.0 copy-start.5
  19.8 0.0 copy-start.6
  19.8 0.0 copy-start.7
  19.8 4.3 %all-to-all-start.1 = ((bf16[4,1184,128]{2,1,0:T(8,128)(2,1)}), bf16[4,1184,128]{2,1,0:T(8,128)(2,1)S(1)}, u32[]{:S(2)}, u32[]{:S(2)}) async-start(bf16[4,1184,128]{2,1,0:T(8,128)(2,1)} %regroup.1.first_ref), calls=%async_computation.1 | async-start | bytes 2424832 | tf_op jit(solution)/shard_map/all_to_all | solution.py:332
  24.1 0.0 collective-permute-done.before_ref
  24.1 0.3 collective-permute-done.1.after_ref
  24.4 0.0 copy-done.5
  24.4 0.0 copy-done.6
  24.4 0.0 copy-done.7
  24.4 16.6 %near.1.near_ref = f32[17,32,256]{2,1,0:T(8,128)S(1)} custom-call(s32[16,16]{1,0:T(8,128)S(1)} %copy-done.6, s32[16]{0:T(128)S(1)} %copy-done.7, bf16[35,4096]{1,0:T(8,128)(2,1)S(1)} %copy-done.5, bf16[35,4096]{1,0:T(8,128)(2,1)S(1)} %collective-permute-done.before_ref, bf16[35,4096]{1,0:T(8,128)(2,1)S(1)} %collective-permute-done.1.after_ref, ...), custom_call_target="tpu_custom_call" | custom-call | flops 16000000000 | bytes 3000000 | tf_op jit(solution)/shard_map/near/pallas_call | solution.py:335
  41.1 0.0 copy-start.2
  41.1 0.0 copy-start.3
  41.1 0.0 all-to-all-done.1.big_ref
  41.1 0.7 coarse.1
  41.8 17.4 %all-to-all-start.2 = ((bf16[32,16,128]{2,1,0:T(8,128)(2,1)}), bf16[32,16,128]{2,1,0:T(8,128)(2,1)S(1)}, u32[]{:S(2)}, u32[]{:S(2)}) async-start(bf16[32,16,128]{2,1,0:T(8,128)(2,1)} %coarse.1), calls=%async_computation.2 | async-start | bytes 262144 | tf_op jit(solution)/shard_map/all_to_all | solution.py:363
  59.8 0.0 copy-done.2
  59.8 0.0 copy-done.3
  59.8 0.0 copy-start
  59.8 0.0 copy-start.1
  59.9 0.0 copy-start.4
  59.9 8.2 %far.1.far_ref = f32[17,32,64]{2,1,0:T(8,128)S(1)} custom-call(s32[16,16]{1,0:T(8,128)S(1)} %copy-done.2, s32[16]{0:T(128)S(1)} %copy-done.3, bf16[4,1184,128]{2,1,0:T(8,128)(2,1)S(1)} %all-to-all-done.1.big_ref, bf16[16,16,64,64]{3,2,1,0:T(8,128)(2,1)} %coupling_ref.1), custom_call_target="tpu_custom_call" | custom-call | flops 1000000000 | bytes 5000000 | tf_op jit(solution)/shard_map/far/pallas_call | solution.py:364
  68.1 4.3 %all-to-all-done.2.coarse_ref = bf16[32,16,128]{2,1,0:T(8,128)(2,1)S(1)} async-done(((bf16[32,16,128]{2,1,0:T(8,128)(2,1)}), bf16[32,16,128]{2,1,0:T(8,128)(2,1)S(1)}, u32[]{:S(2)}, u32[]{:S(2)}) %all-to-all-start.2) | async-done | bytes 131104 | tf_op jit(solution)/shard_map/all_to_all | solution.py:363
  72.3 0.0 copy-done
  72.3 0.0 copy-done.1
  72.3 0.0 copy-done.4
  72.4 3.8 %downward.1 = bf16[32,4096]{1,0:T(8,128)(2,1)} custom-call(s32[1,16]{1,0:T(1,128)S(1)} %copy-done.4, s32[1]{0:T(128)S(6)} %copy.13.count_ref, bf16[32,16,128]{2,1,0:T(8,128)(2,1)S(1)} %all-to-all-done.2.coarse_ref, bf16[4,1184,128]{2,1,0:T(8,128)(2,1)S(1)} %all-to-all-done.1.big_ref, f32[17,32,64]{2,1,0:T(8,128)S(1)} %far.1.far_ref, ...), custom_call_target="tpu_custom_call" | custom-call | flops 100000000 | bytes 3000000 | tf_op jit(solution)/shard_map/downward/pallas_call | solution.py:374
Async XLA Ops:
  2.9 15.7 %all-to-all-start = ((bf16[4,320,128]{2,1,0:T(8,128)(2,1)}), bf16[4,320,128]{2,1,0:T(8,128)(2,1)S(1)}, u32[]{:S(2)}, u32[]{:S(2)}) async-start(bf16[4,320,128]{2,1,0:T(8,128)(2,1)} %get-tuple-element.7), calls=%async_computation | async-start | bytes 655360 | tf_op jit(solution)/shard_map/all_to_all | solution.py:320
  9.9 14.2 %collective-permute-start = (bf16[35,4096]{1,0:T(8,128)(2,1)}, bf16[35,4096]{1,0:T(8,128)(2,1)S(1)}, u32[]{:S(2)}, u32[]{:S(2)}) collective-permute-start(bf16[35,4096]{1,0:T(8,128)(2,1)} %get-tuple-element.8.own_ref), channel_id=1, source_target_pairs={{0,1},{1,2},{2,3},{3,4},{4,5},{5,6},{6,7},{7,8},{8,9},{9,10},{10,1... | collective-permute-start | bytes 860168 | tf_op jit(solution)/shard_map/ppermute | solution.py:321
  13.2 11.3 %collective-permute-start.1 = (bf16[35,4096]{1,0:T(8,128)(2,1)}, bf16[35,4096]{1,0:T(8,128)(2,1)S(1)}, u32[]{:S(2)}, u32[]{:S(2)}) collective-permute-start(bf16[35,4096]{1,0:T(8,128)(2,1)} %get-tuple-element.8.own_ref), channel_id=1, source_target_pairs={{1,0},{2,1},{3,2},{4,3},{5,4},{6,5},{7,6},{8,7},{9,8},{10,9},{11,1... | collective-permute-start | bytes 860168 | tf_op jit(solution)/shard_map/ppermute | solution.py:322
  19.8 4.7 %copy-start.5 = (bf16[35,4096]{1,0:T(8,128)(2,1)S(1)}, bf16[35,4096]{1,0:T(8,128)(2,1)}, u32[]{:S(2)}) copy-start(bf16[35,4096]{1,0:T(8,128)(2,1)} %get-tuple-element.8.own_ref) | copy-start | bytes 860164
  19.8 4.7 %copy-start.6 = (s32[16,16]{1,0:T(8,128)S(1)}, s32[16,16]{1,0:T(8,128)}, u32[]{:S(2)}) copy-start(s32[16,16]{1,0:T(8,128)} %list_ref.3) | copy-start | bytes 3076
  19.8 4.7 %copy-start.7 = (s32[16]{0:T(128)S(1)}, s32[16]{0:T(128)}, u32[]{:S(2)}) copy-start(s32[16]{0:T(128)} %count_ref.3) | copy-start | bytes 196
  19.8 21.3 %all-to-all-start.1 = ((bf16[4,1184,128]{2,1,0:T(8,128)(2,1)}), bf16[4,1184,128]{2,1,0:T(8,128)(2,1)S(1)}, u32[]{:S(2)}, u32[]{:S(2)}) async-start(bf16[4,1184,128]{2,1,0:T(8,128)(2,1)} %regroup.1.first_ref), calls=%async_computation.1 | async-start | bytes 2424832 | tf_op jit(solution)/shard_map/all_to_all | solution.py:332
  41.1 18.7 %copy-start.2 = (s32[16,16]{1,0:T(8,128)S(1)}, s32[16,16]{1,0:T(8,128)}, u32[]{:S(2)}) copy-start(s32[16,16]{1,0:T(8,128)} %list_ref.4) | copy-start | bytes 3076
  41.1 18.7 %copy-start.3 = (s32[16]{0:T(128)S(1)}, s32[16]{0:T(128)}, u32[]{:S(2)}) copy-start(s32[16]{0:T(128)} %count_ref.4) | copy-start | bytes 196
  41.8 30.6 %all-to-all-start.2 = ((bf16[32,16,128]{2,1,0:T(8,128)(2,1)}), bf16[32,16,128]{2,1,0:T(8,128)(2,1)S(1)}, u32[]{:S(2)}, u32[]{:S(2)}) async-start(bf16[32,16,128]{2,1,0:T(8,128)(2,1)} %coarse.1), calls=%async_computation.2 | async-start | bytes 262144 | tf_op jit(solution)/shard_map/all_to_all | solution.py:363
  59.8 12.5 %copy-start = (bf16[16,64,256]{2,1,0:T(8,128)(2,1)S(1)}, bf16[16,64,256]{2,1,0:T(8,128)(2,1)}, u32[]{:S(2)}) copy-start(bf16[16,64,256]{2,1,0:T(8,128)(2,1)} %basis_ref.1) | copy-start | bytes 1572868
  59.8 12.5 %copy-start.1 = (bf16[16,64,64]{2,1,0:T(8,128)(2,1)S(1)}, bf16[16,64,64]{2,1,0:T(8,128)(2,1)}, u32[]{:S(2)}) copy-start(bf16[16,64,64]{2,1,0:T(8,128)(2,1)} %transfer_ref.1) | copy-start | bytes 393220
  59.9 12.5 %copy-start.4 = (s32[1,16]{1,0:T(1,128)S(1)}, s32[1,16]{1,0:T(1,128)}, u32[]{:S(2)}) copy-start(s32[1,16]{1,0:T(1,128)} %list_ref.5) | copy-start | bytes 196

commit v3 on v2

--- a/solution.py
+++ b/solution.py
@@ -10,11 +10,12 @@
 soften = 0.01
 sharpness = inv_four_pi**-2
 feature_depth = 64
-near_at_once = 4
-far_at_once = 8
+near_at_once = 6
+far_at_once = 16
+far_shift = 7
 id_bits = 5
 deep = 4
-vmem_bytes = 50 << 20
+vmem_bytes = 20 << 20
 whole_bytes = 63 << 20
 
 nt_dims = (((1,), (1,)), ((), ()))
@@ -57,10 +58,12 @@
     points = width // leaves
     copies = big_ref.shape[0]
     rows = vecs // 2
-    for copy in copies_in:
-        copy.wait()
+    copies_in[0].wait()
+    copies_in[1].wait()
     halo_ref[0:vecs, :] = vec_ref[...]
     halo_ref[vecs : vecs + off_ref.shape[0], :] = off_ref[...]
+    for copy in copies_in[2:]:
+        copy.wait()
     part = jnp.zeros((vecs, transfer_ref.shape[2]), jnp.float32)
     for i in range(leaves):
         leaf = vec_ref[:, i * points : (i + 1) * points]
@@ -99,14 +102,20 @@
 
 def coarse_kernel(big_ref, near_ref, out_ref):
     members, big_rows = big_ref.shape[:2]
-    rows = out_ref.shape[1]
-    total = jnp.zeros(out_ref.shape[1:], jnp.float32)
+    rows = out_ref.shape[0]
+    total = jnp.zeros(out_ref.shape, jnp.float32)
     for i in range(members):
         high = big_ref[i, big_rows - 2 * rows : big_rows - rows, :].astype(jnp.float32)
         total = total + (high + big_ref[i, big_rows - rows :, :].astype(jnp.float32))
-    rounded = total.astype(jnp.bfloat16)
+    out_ref[...] = total.astype(jnp.bfloat16)
+
+
+def both_kernel(own_ref, other_ref, far_ref, out_ref):
+    rows = own_ref.shape[0]
+    half = lax.axis_index("half")
     for i in range(out_ref.shape[0]):
-        out_ref[i] = rounded
+        out_ref[i, pl.ds(pl.multiple_of(half * rows, rows), rows), :] = own_ref[...]
+        out_ref[i, pl.ds(pl.multiple_of((1 - half) * rows, rows), rows), :] = other_ref[...]
 
 
 def spread(ids, axis_pos):
@@ -123,27 +132,13 @@
     return first, second, (x - first) - second
 
 
-def list_pairs(count_ref, leaves, chunk, put, pad):
-    def one_leaf(t, place):
-        return lax.fori_loop(0, count_ref[t], lambda k, q: put(t, k, q), place)
-
-    total = lax.fori_loop(0, leaves, one_leaf, 0)
-    chunks = (total + chunk - 1) // chunk
-
-    def fill(q, carry):
-        pad(q)
-        return carry
-
-    lax.fori_loop(total, chunks * chunk + chunk, fill, 0)
-    return chunks
-
-
 def near_kernel(
     list_ref, count_ref, own_ref, before_ref, after_ref, first_ref, out_ref, *scratch
 ):
     source, target, vecs, wide, to_leaf, from_leaf, tiles_a, tiles_b = scratch
     leaves = out_ref.shape[0] - 1
     vec_count, width = out_ref.shape[1:]
+    slots = list_ref.shape[1]
     n = leaves * width
     base = list_ref[0, 0]
     rows = lax.broadcasted_iota(jnp.int32, (8, n), 0)
@@ -179,16 +174,20 @@
                 for i in range(leaves):
                     target[i, 16 * j : 16 * (j + 1), :] = block[:, i * width : (i + 1) * width]
 
-    def put(t, k, q):
-        to_leaf[q] = t
-        from_leaf[q] = list_ref[t, k] - base + leaves
-        return q + 1
-
-    def pad(q):
-        to_leaf[q] = leaves
-        from_leaf[q] = 0
-
-    pairs = list_pairs(count_ref, leaves, 2 * near_at_once, put, pad)
+    def one_leaf(t, q):
+        count = count_ref[t]
+        for k in range(slots):
+            to_leaf[q] = t
+            from_leaf[q] = list_ref[t, k] - base + leaves
+            q = q + jnp.where(k < count, 1, 0)
+        return q
+
+    total = lax.fori_loop(0, leaves, one_leaf, 0)
+    for g in range(3 * near_at_once):
+        to_leaf[total + g] = leaves
+        from_leaf[total + g] = 0
+    chunk = 2 * near_at_once
+    chunks = lax.div(total + (chunk - 1), chunk)
     out_ref[...] = jnp.zeros_like(out_ref)
 
     def make_tiles(first, tiles):
@@ -211,46 +210,54 @@
         use_tiles(first + near_at_once, tiles_b)
         return carry
 
-    lax.fori_loop(0, pairs, step, 0)
-
-
-def far_kernel(list_ref, count_ref, big_ref, coupling_ref, out_ref, to_leaf, slot, from_leaf):
+    lax.fori_loop(0, chunks, step, 0)
+
+
+def far_kernel(list_ref, count_ref, big_ref, coupling_ref, first_ref, out_ref, *scratch):
+    to_leaf, pair, from_leaf = scratch
     leaves, slots = coupling_ref.shape[:2]
     across = big_ref.shape[0]
     rows = out_ref.shape[1] // 2
     keep = leaves * rows + coupling_ref.shape[2] // 2
-    group_leaves = across * deep * leaves
-
-    def put(t, k, q):
-        to_leaf[q] = t
-        slot[q] = k
-        from_leaf[q] = lax.rem(list_ref[t, k], group_leaves)
-        return q + 1
-
-    def pad(q):
-        to_leaf[q] = leaves
-        slot[q] = 0
-        from_leaf[q] = 0
-
-    chunks = list_pairs(count_ref, leaves, far_at_once, put, pad)
+    leaf_mask, across_mask = leaves - 1, across - 1
+    leaf_shift, across_shift = leaves.bit_length() - 1, across.bit_length() - 1
+    slot_shift = slots.bit_length() - 1
+
+    def one_leaf(t, q):
+        count = count_ref[t]
+        for k in range(slots):
+            j = jnp.bitwise_and(list_ref[t, k], across * deep * leaves - 1)
+            holder = jnp.right_shift(j, leaf_shift)
+            to_leaf[q] = t
+            pair[q] = t * slots + k
+            place = jnp.right_shift(holder, across_shift) * (keep // rows)
+            place = place + jnp.bitwise_and(j, leaf_mask)
+            from_leaf[q] = jnp.left_shift(jnp.bitwise_and(holder, across_mask), far_shift) + place
+            q = q + jnp.where(k < count, 1, 0)
+        return q
+
+    total = lax.fori_loop(0, leaves, one_leaf, 0)
+    for g in range(far_at_once):
+        to_leaf[total + g] = leaves
+        pair[total + g] = 0
+        from_leaf[total + g] = 0
     out_ref[...] = jnp.zeros_like(out_ref)
 
     def step(i, carry):
         terms = []
         for g in range(far_at_once):
             q = i * far_at_once + g
-            j = from_leaf[q]
-            holder = lax.div(j, leaves)
-            first = lax.div(holder, across) * keep + lax.rem(j, leaves) * rows
+            place = from_leaf[q]
+            first = jnp.bitwise_and(place, (1 << far_shift) - 1) * rows
             first = pl.multiple_of(first, rows)
-            block = unpack(big_ref[lax.rem(holder, across), pl.ds(first, rows), :])
-            coupling = coupling_ref[jnp.minimum(to_leaf[q], leaves - 1), slot[q]]
-            terms.append(dot(block, coupling, nt_dims))
+            block = unpack(big_ref[jnp.right_shift(place, far_shift), pl.ds(first, rows), :])
+            t, k = jnp.right_shift(pair[q], slot_shift), jnp.bitwise_and(pair[q], slots - 1)
+            terms.append(dot(block, coupling_ref[t, k], nt_dims))
         for g, term in enumerate(terms):
             out_ref[to_leaf[i * far_at_once + g]] += term
         return carry
 
-    lax.fori_loop(0, chunks, step, 0)
+    lax.fori_loop(0, lax.div(total + far_at_once - 1, far_at_once), step, 0)
 
 
 def down_kernel(
@@ -259,15 +266,21 @@
     leaves, rank, width = basis_ref.shape
     vec_count = out_ref.shape[0]
     across = big_ref.shape[0]
-    keep = leaves * (vec_count // 2) + rank // 2
-    total = jnp.zeros((vec_count, rank), jnp.float32)
+    rows = vec_count // 2
+    keep = leaves * rows + rank // 2
+    terms = []
     for k in range(list_ref.shape[1]):
-        block = unpack(coarse_ref[list_ref[0, k]])
+        g = list_ref[0, k]
+        peer = jnp.bitwise_and(g, 1) + jnp.left_shift(jnp.right_shift(g, 2), 1)
+        first = pl.multiple_of(jnp.bitwise_and(jnp.right_shift(g, 1), 1) * rows, rows)
+        block = unpack(coarse_ref[peer, pl.ds(first, rows), :])
         block = jnp.where(k < count_ref[0], block, jnp.zeros_like(block))
         last = (k // across + 1) * keep
         coupling = unpack(big_ref[k % across, last - rank // 2 : last, :])
-        total = total + dot(block, coupling, nt_dims)
-    coarse_out = total.astype(jnp.bfloat16)
+        terms.append(dot(block, coupling, nt_dims))
+    while len(terms) > 1:
+        terms = [a + b for a, b in zip(terms[::2], terms[1::2])]
+    coarse_out = terms[0].astype(jnp.bfloat16)
     for i in range(leaves):
         local = far_ref[i] + dot(coarse_out, transfer_ref[i], nt_dims)
         result = near_ref[i] + dot(local.astype(jnp.bfloat16), basis_ref[i], nn_dims)
@@ -294,7 +307,6 @@
 ):
     across = lax.axis_size("across")
     members = lax.axis_size("deep") * across
-    groups = lax.axis_size("grp")
     vec_count, points = vectors.shape
     leaves, rank, width = leaf_basis.shape
     rows = vec_count // 2
@@ -353,24 +365,35 @@
     )(near_list, near_count, halo, before, after, wide)
     coarse = pl.pallas_call(
         coarse_kernel,
-        out_shape=jax.ShapeDtypeStruct((groups, rows, 2 * rank), jnp.bfloat16),
+        out_shape=jax.ShapeDtypeStruct((rows, 2 * rank), jnp.bfloat16),
         in_specs=[vmem, anywhere],
         out_specs=vmem,
         compiler_params=params,
         cost_estimate=cost(40_000, 300_000),
         name="coarse",
     )(big_all, near)
-    coarse_all = lax.all_to_all(coarse, "grp", 0, 0, tiled=True)
+    other = lax.ppermute(coarse, "half", [(0, 1), (1, 0)])
     far = pl.pallas_call(
         far_kernel,
         out_shape=jax.ShapeDtypeStruct((leaves + 1, vec_count, rank), jnp.float32),
-        in_specs=[smem, smem, vmem, vmem],
+        in_specs=[smem, smem, vmem, vmem, anywhere],
         out_specs=vmem,
         scratch_shapes=[pltpu.SMEM((far_pairs,), jnp.int32) for _ in range(3)],
         compiler_params=params,
         cost_estimate=cost(1_000_000_000, 5_000_000),
         name="far",
-    )(far_list, far_count, big_all, leaf_coupling)
+    )(far_list, far_count, big_all, leaf_coupling, coarse)
+    peers = lax.axis_size("row") * lax.axis_size("core")
+    both = pl.pallas_call(
+        both_kernel,
+        out_shape=jax.ShapeDtypeStruct((peers, 2 * rows, 2 * rank), jnp.bfloat16),
+        in_specs=[vmem, vmem, anywhere],
+        out_specs=vmem,
+        compiler_params=params,
+        cost_estimate=cost(40_000, 300_000),
+        name="both",
+    )(coarse, other, far)
+    coarse_all = lax.all_to_all(both, ("row", "core"), 0, 0, tiled=True)
     return pl.pallas_call(
         down_kernel,
         out_shape=jax.ShapeDtypeStruct((vec_count, points), jnp.bfloat16),
@@ -384,9 +407,11 @@
 
 def solution(mesh):
     groups, members = mesh.devices.shape
-    split = Mesh(mesh.devices.reshape(groups, deep, members // deep), ("grp", "deep", "across"))
+    shape = (groups // 4, 2, 2, deep, members // deep)
+    split = Mesh(mesh.devices.reshape(shape), ("row", "half", "core", "deep", "across"))
+    group = ("row", "half", "core")
     leaf = ("deep", "across")
-    both = ("grp",) + leaf
+    both = group + leaf
     placed = (
         P(None, both),
         P(None, both),
@@ -397,8 +422,8 @@
         P(both),
         P(both, None, None, None),
         P(both, None, None),
-        P("grp", None),
-        P("grp"),
-        P("grp", leaf, None, None),
+        P(group, None),
+        P(group),
+        P(group, leaf, None, None),
     )
     return jax.shard_map(body, mesh=split, in_specs=placed, out_specs=P(None, both), check_vma=False)

time: 76.5 us -> 81.3 us (1.063)
  waiting for transfers between devices: 7.95 us -> 12.2 us
  Pallas kernels: 33.4 us -> 29.6 us
  local copies, waits for them, and re-layouts: 0.04 us -> 2.22 us
  starting transfers between devices: 34 us -> 36 us
    ppermute x0 -> x1, starting transfers between devices: none -> 9.78 us  [body(): other = lax.ppermute(coarse, 'half', [(0, 1), (1, 0)])]
    all_to_all x1, starting transfers between devices: 17.4 us -> 9.64 us  [body(): coarse_all = lax.all_to_all(both, ('row', 'core'), 0, 0, tiled=True)]
    all_to_all x1, waiting for transfers between devices: 4.26 us -> 8.52 us  [body(): coarse_all = lax.all_to_all(both, ('row', 'core'), 0, 0, tiled=True)]
    pallas_call x1, Pallas kernels: 8.21 us -> 5.07 us  [body(): pl.pallas_call(far_kernel, out_shape=jax.ShapeDtypeStruct((leaves + 1, ve...]
    unnamed x16 -> x18, local copies, waits for them, and re-layouts: 0.04 us -> 2.22 us
  transfers between devices with their start and end apart: 5 -> 6, of which waited for: 3 -> 3; matrix products, arithmetic and copies ran while one was open for 0% -> 0% of each run, Pallas kernels for 34% -> 27%
where the time goes in v3:
time: 81.3 us; the launch traced here: 80.8 us
  starting transfers between devices  36 us (44%)
  Pallas kernels  29.6 us (36%)
  waiting for transfers between devices  12.2 us (15%)
  local copies, waits for them, and re-layouts  2.22 us (3%)
    pallas_call x1, Pallas kernels, body(): pl.pallas_call(near_kernel, out_shape=jax.ShapeDtypeStruct((leaves + 1, v...  15.9 us
    ppermute x1, starting transfers between devices, body(): other = lax.ppermute(coarse, 'half', [(0, 1), (1, 0)])  9.78 us
    all_to_all x1, starting transfers between devices, body(): coarse_all = lax.all_to_all(both, ('row', 'core'), 0, 0, tiled=True)  9.64 us
    all_to_all x1, waiting for transfers between devices, body(): coarse_all = lax.all_to_all(both, ('row', 'core'), 0, 0, tiled=True)  8.52 us
    all_to_all x1, starting transfers between devices, body(): deep_all = lax.all_to_all(big, 'deep', 0, 0, tiled=True)  6.99 us
    pallas_call x1, Pallas kernels, body(): pl.pallas_call(far_kernel, out_shape=jax.ShapeDtypeStruct((leaves + 1, ve...  5.07 us
    all_to_all x1, starting transfers between devices, body(): big_all = lax.all_to_all(wide, 'across', 0, 0, tiled=True)  4.34 us
    pallas_call x1, Pallas kernels, body(): pl.pallas_call(down_kernel, out_shape=jax.ShapeDtypeStruct((vec_count, po...  3.82 us
  transfers between devices with their start and end apart: 6, of which 3 were waited for; matrix products, arithmetic and copies ran while one was open for 0% of the time, Pallas kernels for 27%

profile of v3, /device:TPU:7, one launch (start us, length us, event | category | flops | bytes accessed | tf_op | source)
XLA Modules:
  0.0 80.8 jit_solution(1152352128106379268)
XLA Ops:
  0.0 2.8 %upward.1 = (bf16[35,4096]{1,0:T(8,128)(2,1)}, bf16[4,320,128]{2,1,0:T(8,128)(2,1)}) custom-call(bf16[32,4096]{1,0:T(8,128)(2,1)} %vec_hbm.1, bf16[3,4096]{1,0:T(4,128)(2,1)} %off_hbm.1, bf16[16,64,256]{2,1,0:T(8,128)(2,1)} %basis_ref.1, bf16[16,64,64]{2,1,0:T(8,128)(2,1)} %transfer_ref.1, bf16[1,1,64,64]{3,2,1,0:T(8,128)(2,1)} %group_hbm.1), custom_call_target="tpu_custom_call" | custom-call | flops 40000000 | bytes 3000000 | tf_op jit(solution)/shard_map/upward/pallas_call | solution.py:318
  2.8 7.0 %all-to-all-start = ((bf16[4,320,128]{2,1,0:T(8,128)(2,1)}), bf16[4,320,128]{2,1,0:T(8,128)(2,1)S(1)}, u32[]{:S(2)}, u32[]{:S(2)}) async-start(bf16[4,320,128]{2,1,0:T(8,128)(2,1)} %get-tuple-element.7), calls=%async_computation | async-start | bytes 655360 | tf_op jit(solution)/shard_map/all_to_all | solution.py:332
  9.8 3.3 %collective-permute-start = (bf16[35,4096]{1,0:T(8,128)(2,1)}, bf16[35,4096]{1,0:T(8,128)(2,1)S(1)}, u32[]{:S(2)}, u32[]{:S(2)}) collective-permute-start(bf16[35,4096]{1,0:T(8,128)(2,1)} %get-tuple-element.8.own_ref), channel_id=1, source_target_pairs={{0,1},{1,2},{2,3},{3,4},{4,5},{5,6},{6,7},{7,8},{8,9},{9,10},{10,1... | collective-permute-start | bytes 860168 | tf_op jit(solution)/shard_map/ppermute | solution.py:333
  13.1 2.0 %collective-permute-start.1 = (bf16[35,4096]{1,0:T(8,128)(2,1)}, bf16[35,4096]{1,0:T(8,128)(2,1)S(1)}, u32[]{:S(2)}, u32[]{:S(2)}) collective-permute-start(bf16[35,4096]{1,0:T(8,128)(2,1)} %get-tuple-element.8.own_ref), channel_id=1, source_target_pairs={{1,0},{2,1},{3,2},{4,3},{5,4},{6,5},{7,6},{8,7},{9,8},{10,9},{11,1... | collective-permute-start | bytes 860168 | tf_op jit(solution)/shard_map/ppermute | solution.py:334
  15.1 3.4 %all-to-all-done.big_ref = bf16[4,320,128]{2,1,0:T(8,128)(2,1)S(1)} async-done(((bf16[4,320,128]{2,1,0:T(8,128)(2,1)}), bf16[4,320,128]{2,1,0:T(8,128)(2,1)S(1)}, u32[]{:S(2)}, u32[]{:S(2)}) %all-to-all-start) | async-done | bytes 327712 | tf_op jit(solution)/shard_map/all_to_all | solution.py:332
  18.5 1.2 %regroup.1.first_ref = bf16[4,1184,128]{2,1,0:T(8,128)(2,1)} custom-call(bf16[4,320,128]{2,1,0:T(8,128)(2,1)S(1)} %all-to-all-done.big_ref), custom_call_target="tpu_custom_call" | custom-call | flops 40000 | bytes 2000000 | tf_op jit(solution)/shard_map/regroup/pallas_call | solution.py:335
  19.7 0.0 copy-start.6
  19.7 0.0 copy-start.7
  19.7 4.3 %all-to-all-start.1 = ((bf16[4,1184,128]{2,1,0:T(8,128)(2,1)}), bf16[4,1184,128]{2,1,0:T(8,128)(2,1)S(1)}, u32[]{:S(2)}, u32[]{:S(2)}) async-start(bf16[4,1184,128]{2,1,0:T(8,128)(2,1)} %regroup.1.first_ref), calls=%async_computation.1 | async-start | bytes 2424832 | tf_op jit(solution)/shard_map/all_to_all | solution.py:344
  24.0 0.0 collective-permute-done.before_ref
  24.1 0.3 collective-permute-done.1.after_ref
  24.4 0.0 copy-done.6
  24.4 0.0 copy-done.7
  24.4 0.0 copy-done.8
  24.4 15.9 %near.1.near_ref = f32[17,32,256]{2,1,0:T(8,128)S(1)} custom-call(s32[16,16]{1,0:T(8,128)S(1)} %copy-done.7, s32[16]{0:T(128)S(1)} %copy-done.8, bf16[35,4096]{1,0:T(8,128)(2,1)S(1)} %copy-done.6, bf16[35,4096]{1,0:T(8,128)(2,1)S(1)} %collective-permute-done.before_ref, bf16[35,4096]{1,0:T(8,128)(2,1)S(1)} %collective-permute-done.1.after_ref, ...), custom_call_target="tpu_custom_call" | custom-call | flops 16000000000 | bytes 3000000 | tf_op jit(solution)/shard_map/near/pallas_call | solution.py:347
  40.3 0.0 copy-start.3
  40.3 0.0 copy-start.4
  40.3 0.0 all-to-all-done.1.big_ref
  40.4 9.8 %collective-permute-start.2 = (bf16[16,128]{1,0:T(8,128)(2,1)S(1)}, bf16[16,128]{1,0:T(8,128)(2,1)S(1)}, u32[]{:S(2)}, u32[]{:S(2)}) collective-permute-start(bf16[16,128]{1,0:T(8,128)(2,1)S(1)} %coarse.1.first_ref.own_ref), channel_id=1, source_target_pairs={{0,32},{32,0},{1,33},{33,1},{2,34},{34,2},{3,35},{35,3},{4,36},{36... | collective-permute-start | bytes 12296 | tf_op jit(solution)/shard_map/ppermute | solution.py:375
  50.2 0.0 copy-done.3
  50.2 0.0 copy-done.4
  50.2 0.0 copy-start
  50.2 2.2 %copy-done = bf16[16,16,64,64]{3,2,1,0:T(8,128)(2,1)S(1)} copy-done((bf16[16,16,64,64]{3,2,1,0:T(8,128)(2,1)S(1)}, bf16[16,16,64,64]{3,2,1,0:T(8,128)(2,1)}, u32[]{:S(2)}) %copy-start) | copy-done | bytes 2097176
  52.4 5.1 %far.1.far_ref = f32[17,32,64]{2,1,0:T(8,128)S(1)} custom-call(s32[16,16]{1,0:T(8,128)S(1)} %copy-done.3, s32[16]{0:T(128)S(1)} %copy-done.4, bf16[4,1184,128]{2,1,0:T(8,128)(2,1)S(1)} %all-to-all-done.1.big_ref, bf16[16,16,64,64]{3,2,1,0:T(8,128)(2,1)S(1)} %copy-done, bf16[16,128]{1,0:T(8,128)(2,1)S(1)} %coarse.1.first_ref.own_ref), custom_call_target="tpu_custom_call" | custom-call | flops 1000000000 | bytes 5000000 | tf_op jit(solution)/shard_map/far/pallas_call | solution.py:376
  57.4 0.0 collective-permute-done.2.other_ref
  57.5 0.7 both.1
  58.1 9.6 %all-to-all-start.2 = ((bf16[16,32,128]{2,1,0:T(8,128)(2,1)}), bf16[16,32,128]{2,1,0:T(8,128)(2,1)S(1)}, u32[]{:S(2)}, u32[]{:S(2)}) async-start(bf16[16,32,128]{2,1,0:T(8,128)(2,1)} %both.1), calls=%async_computation.2 | async-start | bytes 262144 | tf_op jit(solution)/shard_map/all_to_all | solution.py:396
  68.4 8.5 %all-to-all-done.2.coarse_ref = bf16[16,32,128]{2,1,0:T(8,128)(2,1)S(1)} async-done(((bf16[16,32,128]{2,1,0:T(8,128)(2,1)}), bf16[16,32,128]{2,1,0:T(8,128)(2,1)S(1)}, u32[]{:S(2)}, u32[]{:S(2)}) %all-to-all-start.2) | async-done | bytes 131104 | tf_op jit(solution)/shard_map/all_to_all | solution.py:396
  76.9 0.0 copy-done.1
  77.0 0.0 copy-done.2
  77.0 0.0 copy-done.5
  77.0 3.8 %downward.1 = bf16[32,4096]{1,0:T(8,128)(2,1)} custom-call(s32[1,16]{1,0:T(1,128)S(1)} %copy-done.5, s32[1]{0:T(128)S(6)} %copy.13.count_ref, bf16[16,32,128]{2,1,0:T(8,128)(2,1)S(1)} %all-to-all-done.2.coarse_ref, bf16[4,1184,128]{2,1,0:T(8,128)(2,1)S(1)} %all-to-all-done.1.big_ref, f32[17,32,64]{2,1,0:T(8,128)S(1)} %far.1.far_ref, ...), custom_call_target="tpu_custom_call" | custom-call | flops 100000000 | bytes 3000000 | tf_op jit(solution)/shard_map/downward/pallas_call | solution.py:397
  (5 shorter events, 0.0 us)
Async XLA Ops:
  2.8 15.7 %all-to-all-start = ((bf16[4,320,128]{2,1,0:T(8,128)(2,1)}), bf16[4,320,128]{2,1,0:T(8,128)(2,1)S(1)}, u32[]{:S(2)}, u32[]{:S(2)}) async-start(bf16[4,320,128]{2,1,0:T(8,128)(2,1)} %get-tuple-element.7), calls=%async_computation | async-start | bytes 655360 | tf_op jit(solution)/shard_map/all_to_all | solution.py:332
  9.8 14.2 %collective-permute-start = (bf16[35,4096]{1,0:T(8,128)(2,1)}, bf16[35,4096]{1,0:T(8,128)(2,1)S(1)}, u32[]{:S(2)}, u32[]{:S(2)}) collective-permute-start(bf16[35,4096]{1,0:T(8,128)(2,1)} %get-tuple-element.8.own_ref), channel_id=1, source_target_pairs={{0,1},{1,2},{2,3},{3,4},{4,5},{5,6},{6,7},{7,8},{8,9},{9,10},{10,1... | collective-permute-start | bytes 860168 | tf_op jit(solution)/shard_map/ppermute | solution.py:333
  13.1 11.3 %collective-permute-start.1 = (bf16[35,4096]{1,0:T(8,128)(2,1)}, bf16[35,4096]{1,0:T(8,128)(2,1)S(1)}, u32[]{:S(2)}, u32[]{:S(2)}) collective-permute-start(bf16[35,4096]{1,0:T(8,128)(2,1)} %get-tuple-element.8.own_ref), channel_id=1, source_target_pairs={{1,0},{2,1},{3,2},{4,3},{5,4},{6,5},{7,6},{8,7},{9,8},{10,9},{11,1... | collective-permute-start | bytes 860168 | tf_op jit(solution)/shard_map/ppermute | solution.py:334
  19.7 4.7 %copy-start.6 = (bf16[35,4096]{1,0:T(8,128)(2,1)S(1)}, bf16[35,4096]{1,0:T(8,128)(2,1)}, u32[]{:S(2)}) copy-start(bf16[35,4096]{1,0:T(8,128)(2,1)} %get-tuple-element.8.own_ref) | copy-start | bytes 860164
  19.7 4.7 %copy-start.7 = (s32[16,16]{1,0:T(8,128)S(1)}, s32[16,16]{1,0:T(8,128)}, u32[]{:S(2)}) copy-start(s32[16,16]{1,0:T(8,128)} %list_ref.3) | copy-start | bytes 3076
  19.7 4.7 %copy-start.8 = (s32[16]{0:T(128)S(1)}, s32[16]{0:T(128)}, u32[]{:S(2)}) copy-start(s32[16]{0:T(128)} %count_ref.3) | copy-start | bytes 196
  19.7 20.6 %all-to-all-start.1 = ((bf16[4,1184,128]{2,1,0:T(8,128)(2,1)}), bf16[4,1184,128]{2,1,0:T(8,128)(2,1)S(1)}, u32[]{:S(2)}, u32[]{:S(2)}) async-start(bf16[4,1184,128]{2,1,0:T(8,128)(2,1)} %regroup.1.first_ref), calls=%async_computation.1 | async-start | bytes 2424832 | tf_op jit(solution)/shard_map/all_to_all | solution.py:344
  40.3 9.8 %copy-start.3 = (s32[16,16]{1,0:T(8,128)S(1)}, s32[16,16]{1,0:T(8,128)}, u32[]{:S(2)}) copy-start(s32[16,16]{1,0:T(8,128)} %list_ref.4) | copy-start | bytes 3076
  40.3 9.8 %copy-start.4 = (s32[16]{0:T(128)S(1)}, s32[16]{0:T(128)}, u32[]{:S(2)}) copy-start(s32[16]{0:T(128)} %count_ref.4) | copy-start | bytes 196
  40.4 17.1 %collective-permute-start.2 = (bf16[16,128]{1,0:T(8,128)(2,1)S(1)}, bf16[16,128]{1,0:T(8,128)(2,1)S(1)}, u32[]{:S(2)}, u32[]{:S(2)}) collective-permute-start(bf16[16,128]{1,0:T(8,128)(2,1)S(1)} %coarse.1.first_ref.own_ref), channel_id=1, source_target_pairs={{0,32},{32,0},{1,33},{33,1},{2,34},{34,2},{3,35},{35,3},{4,36},{36... | collective-permute-start | bytes 12296 | tf_op jit(solution)/shard_map/ppermute | solution.py:375
  50.2 2.2 %copy-start = (bf16[16,16,64,64]{3,2,1,0:T(8,128)(2,1)S(1)}, bf16[16,16,64,64]{3,2,1,0:T(8,128)(2,1)}, u32[]{:S(2)}) copy-start(bf16[16,16,64,64]{3,2,1,0:T(8,128)(2,1)} %coupling_ref.1) | copy-start | bytes 6291460
  52.4 24.6 %copy-start.1 = (bf16[16,64,256]{2,1,0:T(8,128)(2,1)S(1)}, bf16[16,64,256]{2,1,0:T(8,128)(2,1)}, u32[]{:S(2)}) copy-start(bf16[16,64,256]{2,1,0:T(8,128)(2,1)} %basis_ref.1) | copy-start | bytes 1572868
  52.4 24.6 %copy-start.2 = (bf16[16,64,64]{2,1,0:T(8,128)(2,1)S(1)}, bf16[16,64,64]{2,1,0:T(8,128)(2,1)}, u32[]{:S(2)}) copy-start(bf16[16,64,64]{2,1,0:T(8,128)(2,1)} %transfer_ref.1) | copy-start | bytes 393220
  52.4 24.6 %copy-start.5 = (s32[1,16]{1,0:T(1,128)S(1)}, s32[1,16]{1,0:T(1,128)}, u32[]{:S(2)}) copy-start(s32[1,16]{1,0:T(1,128)} %list_ref.5) | copy-start | bytes 196
  58.1 18.8 %all-to-all-start.2 = ((bf16[16,32,128]{2,1,0:T(8,128)(2,1)}), bf16[16,32,128]{2,1,0:T(8,128)(2,1)S(1)}, u32[]{:S(2)}, u32[]{:S(2)}) async-start(bf16[16,32,128]{2,1,0:T(8,128)(2,1)} %both.1), calls=%async_computation.2 | async-start | bytes 262144 | tf_op jit(solution)/shard_map/all_to_all | solution.py:396

commit v4 on v3

--- a/solution.py
+++ b/solution.py
@@ -102,20 +102,14 @@
 
 def coarse_kernel(big_ref, near_ref, out_ref):
     members, big_rows = big_ref.shape[:2]
-    rows = out_ref.shape[0]
-    total = jnp.zeros(out_ref.shape, jnp.float32)
+    rows = out_ref.shape[1]
+    total = jnp.zeros(out_ref.shape[1:], jnp.float32)
     for i in range(members):
         high = big_ref[i, big_rows - 2 * rows : big_rows - rows, :].astype(jnp.float32)
         total = total + (high + big_ref[i, big_rows - rows :, :].astype(jnp.float32))
-    out_ref[...] = total.astype(jnp.bfloat16)
-
-
-def both_kernel(own_ref, other_ref, far_ref, out_ref):
-    rows = own_ref.shape[0]
-    half = lax.axis_index("half")
+    rounded = total.astype(jnp.bfloat16)
     for i in range(out_ref.shape[0]):
-        out_ref[i, pl.ds(pl.multiple_of(half * rows, rows), rows), :] = own_ref[...]
-        out_ref[i, pl.ds(pl.multiple_of((1 - half) * rows, rows), rows), :] = other_ref[...]
+        out_ref[i] = rounded
 
 
 def spread(ids, axis_pos):
@@ -271,9 +265,8 @@
     terms = []
     for k in range(list_ref.shape[1]):
         g = list_ref[0, k]
-        peer = jnp.bitwise_and(g, 1) + jnp.left_shift(jnp.right_shift(g, 2), 1)
-        first = pl.multiple_of(jnp.bitwise_and(jnp.right_shift(g, 1), 1) * rows, rows)
-        block = unpack(coarse_ref[peer, pl.ds(first, rows), :])
+        low = jnp.bitwise_and(g, 1) * 2 + jnp.bitwise_and(jnp.right_shift(g, 1), 1)
+        block = unpack(coarse_ref[low * (coarse_ref.shape[0] // 4) + jnp.right_shift(g, 2)])
         block = jnp.where(k < count_ref[0], block, jnp.zeros_like(block))
         last = (k // across + 1) * keep
         coupling = unpack(big_ref[k % across, last - rank // 2 : last, :])
@@ -307,6 +300,7 @@
 ):
     across = lax.axis_size("across")
     members = lax.axis_size("deep") * across
+    groups = lax.axis_size("row") * 4
     vec_count, points = vectors.shape
     leaves, rank, width = leaf_basis.shape
     rows = vec_count // 2
@@ -365,14 +359,14 @@
     )(near_list, near_count, halo, before, after, wide)
     coarse = pl.pallas_call(
         coarse_kernel,
-        out_shape=jax.ShapeDtypeStruct((rows, 2 * rank), jnp.bfloat16),
+        out_shape=jax.ShapeDtypeStruct((groups, rows, 2 * rank), jnp.bfloat16),
         in_specs=[vmem, anywhere],
         out_specs=vmem,
         compiler_params=params,
         cost_estimate=cost(40_000, 300_000),
         name="coarse",
     )(big_all, near)
-    other = lax.ppermute(coarse, "half", [(0, 1), (1, 0)])
+    coarse_all = lax.all_to_all(coarse, ("core", "half", "row"), 0, 0, tiled=True)
     far = pl.pallas_call(
         far_kernel,
         out_shape=jax.ShapeDtypeStruct((leaves + 1, vec_count, rank), jnp.float32),
@@ -383,17 +377,6 @@
         cost_estimate=cost(1_000_000_000, 5_000_000),
         name="far",
     )(far_list, far_count, big_all, leaf_coupling, coarse)
-    peers = lax.axis_size("row") * lax.axis_size("core")
-    both = pl.pallas_call(
-        both_kernel,
-        out_shape=jax.ShapeDtypeStruct((peers, 2 * rows, 2 * rank), jnp.bfloat16),
-        in_specs=[vmem, vmem, anywhere],
-        out_specs=vmem,
-        compiler_params=params,
-        cost_estimate=cost(40_000, 300_000),
-        name="both",
-    )(coarse, other, far)
-    coarse_all = lax.all_to_all(both, ("row", "core"), 0, 0, tiled=True)
     return pl.pallas_call(
         down_kernel,
         out_shape=jax.ShapeDtypeStruct((vec_count, points), jnp.bfloat16),

time: 81.3 us -> 75.6 us (0.930)
  waiting for transfers between devices: 12.2 us -> 8.75 us
  starting transfers between devices: 36 us -> 34.1 us
  Pallas kernels: 29.6 us -> 28.5 us
    ppermute x1 -> x0, starting transfers between devices: 9.78 us -> none  [body(): other = lax.ppermute(coarse, 'half', [(0, 1), (1, 0)])]
    all_to_all x1, starting transfers between devices: 9.64 us -> 17.5 us  [body(): lax.all_to_all(coarse, ('core', 'half', 'row'), 0, 0, tiled=True)]
    all_to_all x1, waiting for transfers between devices: 8.52 us -> 5.05 us  [body(): lax.all_to_all(coarse, ('core', 'half', 'row'), 0, 0, tiled=True)]
  transfers between devices with their start and end apart: 6 -> 5, of which waited for: 3 -> 3; matrix products, arithmetic and copies ran while one was open for 0% -> 0% of each run, Pallas kernels for 27% -> 28%
where the time goes in v4:
time: 75.6 us; the launch traced here: 74.3 us
  starting transfers between devices  34.1 us (45%)
  Pallas kernels  28.5 us (38%)
  waiting for transfers between devices  8.75 us (12%)
  local copies, waits for them, and re-layouts  2.22 us (3%)
    all_to_all x1, starting transfers between devices, body(): lax.all_to_all(coarse, ('core', 'half', 'row'), 0, 0, tiled=True)  17.5 us
    pallas_call x1, Pallas kernels, body(): pl.pallas_call(near_kernel, out_shape=jax.ShapeDtypeStruct((leaves + 1, v...  15.2 us
    all_to_all x1, starting transfers between devices, body(): deep_all = lax.all_to_all(big, 'deep', 0, 0, tiled=True)  6.99 us
    all_to_all x1, waiting for transfers between devices, body(): lax.all_to_all(coarse, ('core', 'half', 'row'), 0, 0, tiled=True)  5.05 us
    pallas_call x1, Pallas kernels, body(): pl.pallas_call(far_kernel, out_shape=jax.ShapeDtypeStruct((leaves + 1, ve...  4.76 us
    all_to_all x1, starting transfers between devices, body(): big_all = lax.all_to_all(wide, 'across', 0, 0, tiled=True)  4.34 us
    pallas_call x1, Pallas kernels, body(): pl.pallas_call(down_kernel, out_shape=jax.ShapeDtypeStruct((vec_count, po...  3.82 us
    all_to_all x1, waiting for transfers between devices, body(): deep_all = lax.all_to_all(big, 'deep', 0, 0, tiled=True)  3.37 us
  transfers between devices with their start and end apart: 5, of which 3 were waited for; matrix products, arithmetic and copies ran while one was open for 0% of the time, Pallas kernels for 28%

profile of v4, /device:TPU:7, one launch (start us, length us, event | category | flops | bytes accessed | tf_op | source)
XLA Modules:
  0.0 74.3 jit_solution(6141862947743713470)
XLA Ops:
  0.0 2.8 %upward.1 = (bf16[35,4096]{1,0:T(8,128)(2,1)}, bf16[4,320,128]{2,1,0:T(8,128)(2,1)}) custom-call(bf16[32,4096]{1,0:T(8,128)(2,1)} %vec_hbm.1, bf16[3,4096]{1,0:T(4,128)(2,1)} %off_hbm.1, bf16[16,64,256]{2,1,0:T(8,128)(2,1)} %basis_ref.1, bf16[16,64,64]{2,1,0:T(8,128)(2,1)} %transfer_ref.1, bf16[1,1,64,64]{3,2,1,0:T(8,128)(2,1)} %group_hbm.1), custom_call_target="tpu_custom_call" | custom-call | flops 40000000 | bytes 3000000 | tf_op jit(solution)/shard_map/upward/pallas_call | solution.py:312
  2.8 7.0 %all-to-all-start = ((bf16[4,320,128]{2,1,0:T(8,128)(2,1)}), bf16[4,320,128]{2,1,0:T(8,128)(2,1)S(1)}, u32[]{:S(2)}, u32[]{:S(2)}) async-start(bf16[4,320,128]{2,1,0:T(8,128)(2,1)} %get-tuple-element.7), calls=%async_computation | async-start | bytes 655360 | tf_op jit(solution)/shard_map/all_to_all | solution.py:326
  9.8 3.3 %collective-permute-start = (bf16[35,4096]{1,0:T(8,128)(2,1)}, bf16[35,4096]{1,0:T(8,128)(2,1)S(1)}, u32[]{:S(2)}, u32[]{:S(2)}) collective-permute-start(bf16[35,4096]{1,0:T(8,128)(2,1)} %get-tuple-element.8.own_ref), channel_id=1, source_target_pairs={{0,1},{1,2},{2,3},{3,4},{4,5},{5,6},{6,7},{7,8},{8,9},{9,10},{10,1... | collective-permute-start | bytes 860168 | tf_op jit(solution)/shard_map/ppermute | solution.py:327
  13.1 2.0 %collective-permute-start.1 = (bf16[35,4096]{1,0:T(8,128)(2,1)}, bf16[35,4096]{1,0:T(8,128)(2,1)S(1)}, u32[]{:S(2)}, u32[]{:S(2)}) collective-permute-start(bf16[35,4096]{1,0:T(8,128)(2,1)} %get-tuple-element.8.own_ref), channel_id=1, source_target_pairs={{1,0},{2,1},{3,2},{4,3},{5,4},{6,5},{7,6},{8,7},{9,8},{10,9},{11,1... | collective-permute-start | bytes 860168 | tf_op jit(solution)/shard_map/ppermute | solution.py:328
  15.1 3.4 %all-to-all-done.big_ref = bf16[4,320,128]{2,1,0:T(8,128)(2,1)S(1)} async-done(((bf16[4,320,128]{2,1,0:T(8,128)(2,1)}), bf16[4,320,128]{2,1,0:T(8,128)(2,1)S(1)}, u32[]{:S(2)}, u32[]{:S(2)}) %all-to-all-start) | async-done | bytes 327712 | tf_op jit(solution)/shard_map/all_to_all | solution.py:326
  18.5 1.2 %regroup.1.first_ref = bf16[4,1184,128]{2,1,0:T(8,128)(2,1)} custom-call(bf16[4,320,128]{2,1,0:T(8,128)(2,1)S(1)} %all-to-all-done.big_ref), custom_call_target="tpu_custom_call" | custom-call | flops 40000 | bytes 2000000 | tf_op jit(solution)/shard_map/regroup/pallas_call | solution.py:329
  19.7 0.0 copy-start.6
  19.7 0.0 copy-start.7
  19.7 0.0 copy-start.8
  19.7 4.3 %all-to-all-start.1 = ((bf16[4,1184,128]{2,1,0:T(8,128)(2,1)}), bf16[4,1184,128]{2,1,0:T(8,128)(2,1)S(1)}, u32[]{:S(2)}, u32[]{:S(2)}) async-start(bf16[4,1184,128]{2,1,0:T(8,128)(2,1)} %regroup.1.first_ref), calls=%async_computation.1 | async-start | bytes 2424832 | tf_op jit(solution)/shard_map/all_to_all | solution.py:338
  24.0 0.0 collective-permute-done.before_ref
  24.0 0.3 collective-permute-done.1.after_ref
  24.4 0.0 copy-done.6
  24.4 0.0 copy-done.7
  24.4 0.0 copy-done.8
  24.4 15.2 %near.1.near_ref = f32[17,32,256]{2,1,0:T(8,128)S(1)} custom-call(s32[16,16]{1,0:T(8,128)S(1)} %copy-done.7, s32[16]{0:T(128)S(1)} %copy-done.8, bf16[35,4096]{1,0:T(8,128)(2,1)S(1)} %copy-done.6, bf16[35,4096]{1,0:T(8,128)(2,1)S(1)} %collective-permute-done.before_ref, bf16[35,4096]{1,0:T(8,128)(2,1)S(1)} %collective-permute-done.1.after_ref, ...), custom_call_target="tpu_custom_call" | custom-call | flops 16000000000 | bytes 3000000 | tf_op jit(solution)/shard_map/near/pallas_call | solution.py:341
  39.6 0.0 copy-start.3
  39.6 0.0 copy-start.4
  39.6 0.0 all-to-all-done.1.big_ref
  39.6 0.7 coarse.1.first_ref
  40.3 17.5 %all-to-all-start.2 = ((bf16[32,16,128]{2,1,0:T(8,128)(2,1)}), bf16[32,16,128]{2,1,0:T(8,128)(2,1)S(1)}, u32[]{:S(2)}, u32[]{:S(2)}) async-start(bf16[32,16,128]{2,1,0:T(8,128)(2,1)} %coarse.1.first_ref), calls=%async_computation.2 | async-start | bytes 262144 | tf_op jit(solution)/shard_map/all_to_all | solution.py:369
  58.5 0.0 copy-done.3
  58.5 0.0 copy-done.4
  58.5 0.0 copy-start
  58.5 2.2 %copy-done = bf16[16,16,64,64]{3,2,1,0:T(8,128)(2,1)S(1)} copy-done((bf16[16,16,64,64]{3,2,1,0:T(8,128)(2,1)S(1)}, bf16[16,16,64,64]{3,2,1,0:T(8,128)(2,1)}, u32[]{:S(2)}) %copy-start) | copy-done | bytes 2097176
  60.7 0.0 copy-start.1
  60.7 4.8 %far.1.far_ref = f32[17,32,64]{2,1,0:T(8,128)S(1)} custom-call(s32[16,16]{1,0:T(8,128)S(1)} %copy-done.3, s32[16]{0:T(128)S(1)} %copy-done.4, bf16[4,1184,128]{2,1,0:T(8,128)(2,1)S(1)} %all-to-all-done.1.big_ref, bf16[16,16,64,64]{3,2,1,0:T(8,128)(2,1)S(1)} %copy-done, bf16[32,16,128]{2,1,0:T(8,128)(2,1)} %coarse.1.first_ref), custom_call_target="tpu_custom_call" | custom-call | flops 1000000000 | bytes 5000000 | tf_op jit(solution)/shard_map/far/pallas_call | solution.py:370
  65.4 5.1 %all-to-all-done.2.coarse_ref = bf16[32,16,128]{2,1,0:T(8,128)(2,1)S(1)} async-done(((bf16[32,16,128]{2,1,0:T(8,128)(2,1)}), bf16[32,16,128]{2,1,0:T(8,128)(2,1)S(1)}, u32[]{:S(2)}, u32[]{:S(2)}) %all-to-all-start.2) | async-done | bytes 131104 | tf_op jit(solution)/shard_map/all_to_all | solution.py:369
  70.5 0.0 copy-done.1
  70.5 0.0 copy-done.2
  70.5 0.0 copy-done.5
  70.5 3.8 %downward.1 = bf16[32,4096]{1,0:T(8,128)(2,1)} custom-call(s32[1,16]{1,0:T(1,128)S(1)} %copy-done.5, s32[1]{0:T(128)S(6)} %copy.13.count_ref, bf16[32,16,128]{2,1,0:T(8,128)(2,1)S(1)} %all-to-all-done.2.coarse_ref, bf16[4,1184,128]{2,1,0:T(8,128)(2,1)S(1)} %all-to-all-done.1.big_ref, f32[17,32,64]{2,1,0:T(8,128)S(1)} %far.1.far_ref, ...), custom_call_target="tpu_custom_call" | custom-call | flops 100000000 | bytes 3000000 | tf_op jit(solution)/shard_map/downward/pallas_call | solution.py:380
  (2 shorter events, 0.0 us)
Async XLA Ops:
  2.8 15.7 %all-to-all-start = ((bf16[4,320,128]{2,1,0:T(8,128)(2,1)}), bf16[4,320,128]{2,1,0:T(8,128)(2,1)S(1)}, u32[]{:S(2)}, u32[]{:S(2)}) async-start(bf16[4,320,128]{2,1,0:T(8,128)(2,1)} %get-tuple-element.7), calls=%async_computation | async-start | bytes 655360 | tf_op jit(solution)/shard_map/all_to_all | solution.py:326
  9.8 14.2 %collective-permute-start = (bf16[35,4096]{1,0:T(8,128)(2,1)}, bf16[35,4096]{1,0:T(8,128)(2,1)S(1)}, u32[]{:S(2)}, u32[]{:S(2)}) collective-permute-start(bf16[35,4096]{1,0:T(8,128)(2,1)} %get-tuple-element.8.own_ref), channel_id=1, source_target_pairs={{0,1},{1,2},{2,3},{3,4},{4,5},{5,6},{6,7},{7,8},{8,9},{9,10},{10,1... | collective-permute-start | bytes 860168 | tf_op jit(solution)/shard_map/ppermute | solution.py:327
  13.1 11.3 %collective-permute-start.1 = (bf16[35,4096]{1,0:T(8,128)(2,1)}, bf16[35,4096]{1,0:T(8,128)(2,1)S(1)}, u32[]{:S(2)}, u32[]{:S(2)}) collective-permute-start(bf16[35,4096]{1,0:T(8,128)(2,1)} %get-tuple-element.8.own_ref), channel_id=1, source_target_pairs={{1,0},{2,1},{3,2},{4,3},{5,4},{6,5},{7,6},{8,7},{9,8},{10,9},{11,1... | collective-permute-start | bytes 860168 | tf_op jit(solution)/shard_map/ppermute | solution.py:328
  19.7 4.7 %copy-start.6 = (bf16[35,4096]{1,0:T(8,128)(2,1)S(1)}, bf16[35,4096]{1,0:T(8,128)(2,1)}, u32[]{:S(2)}) copy-start(bf16[35,4096]{1,0:T(8,128)(2,1)} %get-tuple-element.8.own_ref) | copy-start | bytes 860164
  19.7 4.7 %copy-start.7 = (s32[16,16]{1,0:T(8,128)S(1)}, s32[16,16]{1,0:T(8,128)}, u32[]{:S(2)}) copy-start(s32[16,16]{1,0:T(8,128)} %list_ref.3) | copy-start | bytes 3076
  19.7 4.7 %copy-start.8 = (s32[16]{0:T(128)S(1)}, s32[16]{0:T(128)}, u32[]{:S(2)}) copy-start(s32[16]{0:T(128)} %count_ref.3) | copy-start | bytes 196
  19.7 19.9 %all-to-all-start.1 = ((bf16[4,1184,128]{2,1,0:T(8,128)(2,1)}), bf16[4,1184,128]{2,1,0:T(8,128)(2,1)S(1)}, u32[]{:S(2)}, u32[]{:S(2)}) async-start(bf16[4,1184,128]{2,1,0:T(8,128)(2,1)} %regroup.1.first_ref), calls=%async_computation.1 | async-start | bytes 2424832 | tf_op jit(solution)/shard_map/all_to_all | solution.py:338
  39.6 18.9 %copy-start.3 = (s32[16,16]{1,0:T(8,128)S(1)}, s32[16,16]{1,0:T(8,128)}, u32[]{:S(2)}) copy-start(s32[16,16]{1,0:T(8,128)} %list_ref.4) | copy-start | bytes 3076
  39.6 18.9 %copy-start.4 = (s32[16]{0:T(128)S(1)}, s32[16]{0:T(128)}, u32[]{:S(2)}) copy-start(s32[16]{0:T(128)} %count_ref.4) | copy-start | bytes 196
  40.3 30.2 %all-to-all-start.2 = ((bf16[32,16,128]{2,1,0:T(8,128)(2,1)}), bf16[32,16,128]{2,1,0:T(8,128)(2,1)S(1)}, u32[]{:S(2)}, u32[]{:S(2)}) async-start(bf16[32,16,128]{2,1,0:T(8,128)(2,1)} %coarse.1.first_ref), calls=%async_computation.2 | async-start | bytes 262144 | tf_op jit(solution)/shard_map/all_to_all | solution.py:369
  58.5 2.2 %copy-start = (bf16[16,16,64,64]{3,2,1,0:T(8,128)(2,1)S(1)}, bf16[16,16,64,64]{3,2,1,0:T(8,128)(2,1)}, u32[]{:S(2)}) copy-start(bf16[16,16,64,64]{3,2,1,0:T(8,128)(2,1)} %coupling_ref.1) | copy-start | bytes 6291460
  60.7 9.8 %copy-start.1 = (bf16[16,64,256]{2,1,0:T(8,128)(2,1)S(1)}, bf16[16,64,256]{2,1,0:T(8,128)(2,1)}, u32[]{:S(2)}) copy-start(bf16[16,64,256]{2,1,0:T(8,128)(2,1)} %basis_ref.1) | copy-start | bytes 1572868
  60.7 9.8 %copy-start.2 = (bf16[16,64,64]{2,1,0:T(8,128)(2,1)S(1)}, bf16[16,64,64]{2,1,0:T(8,128)(2,1)}, u32[]{:S(2)}) copy-start(bf16[16,64,64]{2,1,0:T(8,128)(2,1)} %transfer_ref.1) | copy-start | bytes 393220
  60.7 9.8 %copy-start.5 = (s32[1,16]{1,0:T(1,128)S(1)}, s32[1,16]{1,0:T(1,128)}, u32[]{:S(2)}) copy-start(s32[1,16]{1,0:T(1,128)} %list_ref.5) | copy-start | bytes 196

commit v5 on v4

--- a/solution.py
+++ b/solution.py
@@ -64,14 +64,16 @@
     halo_ref[vecs : vecs + off_ref.shape[0], :] = off_ref[...]
     for copy in copies_in[2:]:
         copy.wait()
-    part = jnp.zeros((vecs, transfer_ref.shape[2]), jnp.float32)
+    coeffs = []
     for i in range(leaves):
         leaf = vec_ref[:, i * points : (i + 1) * points]
         coeff = dot(leaf, basis_ref[i], nt_dims).astype(jnp.bfloat16)
-        part = part + dot(coeff, transfer_ref[i], nn_dims)
+        coeffs.append(coeff)
         packed = pack(coeff)
         for c in range(copies):
             big_ref[c, i * rows : (i + 1) * rows, :] = packed
+    stacked = transfer_ref[...].reshape(leaves * transfer_ref.shape[1], transfer_ref.shape[2])
+    part = dot(jnp.concatenate(coeffs, axis=1), stacked, nn_dims)
     coupling = pack(group_ref[0, 0])
     packed_part = pack(part)
     high = packed_part.astype(jnp.bfloat16)
@@ -274,8 +276,10 @@
     while len(terms) > 1:
         terms = [a + b for a, b in zip(terms[::2], terms[1::2])]
     coarse_out = terms[0].astype(jnp.bfloat16)
+    stacked = transfer_ref[...].reshape(leaves * rank, transfer_ref.shape[2])
+    downward = dot(coarse_out, stacked, nt_dims)
     for i in range(leaves):
-        local = far_ref[i] + dot(coarse_out, transfer_ref[i], nt_dims)
+        local = far_ref[i] + downward[:, i * rank : (i + 1) * rank]
         result = near_ref[i] + dot(local.astype(jnp.bfloat16), basis_ref[i], nn_dims)
         out_ref[:, i * width : (i + 1) * width] = result.astype(jnp.bfloat16)
 

time: 75.6 us -> 73.6 us (0.974)
  Pallas kernels: 28.5 us -> 26.7 us
    pallas_call x1, Pallas kernels: 3.82 us -> 2.12 us  [body(): pl.pallas_call(down_kernel, out_shape=jax.ShapeDtypeStruct((vec_count, po...]
  transfers between devices with their start and end apart: 5 -> 5, of which waited for: 3 -> 3; matrix products, arithmetic and copies ran while one was open for 0% -> 0% of each run, Pallas kernels for 28% -> 30%
where the time goes in v5:
time: 73.6 us; the launch traced here: 72.3 us
  starting transfers between devices  34.1 us (46%)
  Pallas kernels  26.7 us (36%)
  waiting for transfers between devices  8.44 us (11%)
  local copies, waits for them, and re-layouts  2.22 us (3%)
  between operations  0.75 us (1%)
    all_to_all x1, starting transfers between devices, body(): lax.all_to_all(coarse, ('core', 'half', 'row'), 0, 0, tiled=True)  17.6 us
    pallas_call x1, Pallas kernels, body(): pl.pallas_call(near_kernel, out_shape=jax.ShapeDtypeStruct((leaves + 1, v...  15.2 us
    all_to_all x1, starting transfers between devices, body(): deep_all = lax.all_to_all(big, 'deep', 0, 0, tiled=True)  6.99 us
    pallas_call x1, Pallas kernels, body(): pl.pallas_call(far_kernel, out_shape=jax.ShapeDtypeStruct((leaves + 1, ve...  5.07 us
    all_to_all x1, waiting for transfers between devices, body(): lax.all_to_all(coarse, ('core', 'half', 'row'), 0, 0, tiled=True)  4.74 us
    all_to_all x1, starting transfers between devices, body(): big_all = lax.all_to_all(wide, 'across', 0, 0, tiled=True)  4.34 us
    all_to_all x1, waiting for transfers between devices, body(): deep_all = lax.all_to_all(big, 'deep', 0, 0, tiled=True)  3.37 us
    ppermute x1, starting transfers between devices, body(): before = lax.ppermute(halo, ('deep', 'across'), up)  3.27 us
  transfers between devices with their start and end apart: 5, of which 3 were waited for; matrix products, arithmetic and copies ran while one was open for 0% of the time, Pallas kernels for 30%

profile of v5, /device:TPU:7, one launch (start us, length us, event | category | flops | bytes accessed | tf_op | source)
XLA Modules:
  0.0 72.3 jit_solution(648047206711848858)
XLA Ops:
  0.0 2.5 %upward.1 = (bf16[35,4096]{1,0:T(8,128)(2,1)}, bf16[4,320,128]{2,1,0:T(8,128)(2,1)}) custom-call(bf16[32,4096]{1,0:T(8,128)(2,1)} %vec_hbm.1, bf16[3,4096]{1,0:T(4,128)(2,1)} %off_hbm.1, bf16[16,64,256]{2,1,0:T(8,128)(2,1)} %basis_ref.1, bf16[16,64,64]{2,1,0:T(8,128)(2,1)} %transfer_ref.1, bf16[1,1,64,64]{3,2,1,0:T(8,128)(2,1)} %group_hbm.1), custom_call_target="tpu_custom_call" | custom-call | flops 40000000 | bytes 3000000 | tf_op jit(solution)/shard_map/upward/pallas_call | solution.py:316
  2.5 7.0 %all-to-all-start = ((bf16[4,320,128]{2,1,0:T(8,128)(2,1)}), bf16[4,320,128]{2,1,0:T(8,128)(2,1)S(1)}, u32[]{:S(2)}, u32[]{:S(2)}) async-start(bf16[4,320,128]{2,1,0:T(8,128)(2,1)} %get-tuple-element.7), calls=%async_computation | async-start | bytes 655360 | tf_op jit(solution)/shard_map/all_to_all | solution.py:330
  9.5 3.3 %collective-permute-start = (bf16[35,4096]{1,0:T(8,128)(2,1)}, bf16[35,4096]{1,0:T(8,128)(2,1)S(1)}, u32[]{:S(2)}, u32[]{:S(2)}) collective-permute-start(bf16[35,4096]{1,0:T(8,128)(2,1)} %get-tuple-element.8.own_ref), channel_id=1, source_target_pairs={{0,1},{1,2},{2,3},{3,4},{4,5},{5,6},{6,7},{7,8},{8,9},{9,10},{10,1... | collective-permute-start | bytes 860168 | tf_op jit(solution)/shard_map/ppermute | solution.py:331
  12.8 2.0 %collective-permute-start.1 = (bf16[35,4096]{1,0:T(8,128)(2,1)}, bf16[35,4096]{1,0:T(8,128)(2,1)S(1)}, u32[]{:S(2)}, u32[]{:S(2)}) collective-permute-start(bf16[35,4096]{1,0:T(8,128)(2,1)} %get-tuple-element.8.own_ref), channel_id=1, source_target_pairs={{1,0},{2,1},{3,2},{4,3},{5,4},{6,5},{7,6},{8,7},{9,8},{10,9},{11,1... | collective-permute-start | bytes 860168 | tf_op jit(solution)/shard_map/ppermute | solution.py:332
  14.8 3.4 %all-to-all-done.big_ref = bf16[4,320,128]{2,1,0:T(8,128)(2,1)S(1)} async-done(((bf16[4,320,128]{2,1,0:T(8,128)(2,1)}), bf16[4,320,128]{2,1,0:T(8,128)(2,1)S(1)}, u32[]{:S(2)}, u32[]{:S(2)}) %all-to-all-start) | async-done | bytes 327712 | tf_op jit(solution)/shard_map/all_to_all | solution.py:330
  18.2 1.2 %regroup.1.first_ref = bf16[4,1184,128]{2,1,0:T(8,128)(2,1)} custom-call(bf16[4,320,128]{2,1,0:T(8,128)(2,1)S(1)} %all-to-all-done.big_ref), custom_call_target="tpu_custom_call" | custom-call | flops 40000 | bytes 2000000 | tf_op jit(solution)/shard_map/regroup/pallas_call | solution.py:333
  19.4 0.0 copy-start.6
  19.4 0.0 copy-start.7
  19.4 0.0 copy-start.8
  19.4 4.3 %all-to-all-start.1 = ((bf16[4,1184,128]{2,1,0:T(8,128)(2,1)}), bf16[4,1184,128]{2,1,0:T(8,128)(2,1)S(1)}, u32[]{:S(2)}, u32[]{:S(2)}) async-start(bf16[4,1184,128]{2,1,0:T(8,128)(2,1)} %regroup.1.first_ref), calls=%async_computation.1 | async-start | bytes 2424832 | tf_op jit(solution)/shard_map/all_to_all | solution.py:342
  23.7 0.0 collective-permute-done.before_ref
  23.7 0.3 collective-permute-done.1.after_ref
  24.0 0.0 copy-done.6
  24.0 0.0 copy-done.7
  24.0 0.0 copy-done.8
  24.0 15.2 %near.1.near_ref = f32[17,32,256]{2,1,0:T(8,128)S(1)} custom-call(s32[16,16]{1,0:T(8,128)S(1)} %copy-done.7, s32[16]{0:T(128)S(1)} %copy-done.8, bf16[35,4096]{1,0:T(8,128)(2,1)S(1)} %copy-done.6, bf16[35,4096]{1,0:T(8,128)(2,1)S(1)} %collective-permute-done.before_ref, bf16[35,4096]{1,0:T(8,128)(2,1)S(1)} %collective-permute-done.1.after_ref, ...), custom_call_target="tpu_custom_call" | custom-call | flops 16000000000 | bytes 3000000 | tf_op jit(solution)/shard_map/near/pallas_call | solution.py:345
  39.2 0.0 copy-start.3
  39.2 0.0 copy-start.4
  39.2 0.0 all-to-all-done.1.big_ref
  39.3 0.7 coarse.1.first_ref
  39.9 17.6 %all-to-all-start.2 = ((bf16[32,16,128]{2,1,0:T(8,128)(2,1)}), bf16[32,16,128]{2,1,0:T(8,128)(2,1)S(1)}, u32[]{:S(2)}, u32[]{:S(2)}) async-start(bf16[32,16,128]{2,1,0:T(8,128)(2,1)} %coarse.1.first_ref), calls=%async_computation.2 | async-start | bytes 262144 | tf_op jit(solution)/shard_map/all_to_all | solution.py:373
  58.1 0.0 copy-done.3
  58.1 0.0 copy-done.4
  58.1 0.0 copy-start
  58.2 2.2 %copy-done = bf16[16,16,64,64]{3,2,1,0:T(8,128)(2,1)S(1)} copy-done((bf16[16,16,64,64]{3,2,1,0:T(8,128)(2,1)S(1)}, bf16[16,16,64,64]{3,2,1,0:T(8,128)(2,1)}, u32[]{:S(2)}) %copy-start) | copy-done | bytes 2097176
  60.3 0.0 copy-start.1
  60.3 5.1 %far.1.far_ref = f32[17,32,64]{2,1,0:T(8,128)S(1)} custom-call(s32[16,16]{1,0:T(8,128)S(1)} %copy-done.3, s32[16]{0:T(128)S(1)} %copy-done.4, bf16[4,1184,128]{2,1,0:T(8,128)(2,1)S(1)} %all-to-all-done.1.big_ref, bf16[16,16,64,64]{3,2,1,0:T(8,128)(2,1)S(1)} %copy-done, bf16[32,16,128]{2,1,0:T(8,128)(2,1)} %coarse.1.first_ref), custom_call_target="tpu_custom_call" | custom-call | flops 1000000000 | bytes 5000000 | tf_op jit(solution)/shard_map/far/pallas_call | solution.py:374
  65.4 4.7 %all-to-all-done.2.coarse_ref = bf16[32,16,128]{2,1,0:T(8,128)(2,1)S(1)} async-done(((bf16[32,16,128]{2,1,0:T(8,128)(2,1)}), bf16[32,16,128]{2,1,0:T(8,128)(2,1)S(1)}, u32[]{:S(2)}, u32[]{:S(2)}) %all-to-all-start.2) | async-done | bytes 131104 | tf_op jit(solution)/shard_map/all_to_all | solution.py:373
  70.2 0.0 copy-done.1
  70.2 0.0 copy-done.2
  70.2 0.0 copy-done.5
  70.2 2.1 %downward.1 = bf16[32,4096]{1,0:T(8,128)(2,1)} custom-call(s32[1,16]{1,0:T(1,128)S(1)} %copy-done.5, s32[1]{0:T(128)S(6)} %copy.13.count_ref, bf16[32,16,128]{2,1,0:T(8,128)(2,1)S(1)} %all-to-all-done.2.coarse_ref, bf16[4,1184,128]{2,1,0:T(8,128)(2,1)S(1)} %all-to-all-done.1.big_ref, f32[17,32,64]{2,1,0:T(8,128)S(1)} %far.1.far_ref, ...), custom_call_target="tpu_custom_call" | custom-call | flops 100000000 | bytes 3000000 | tf_op jit(solution)/shard_map/downward/pallas_call | solution.py:384
  (2 shorter events, 0.0 us)
Async XLA Ops:
  2.5 15.6 %all-to-all-start = ((bf16[4,320,128]{2,1,0:T(8,128)(2,1)}), bf16[4,320,128]{2,1,0:T(8,128)(2,1)S(1)}, u32[]{:S(2)}, u32[]{:S(2)}) async-start(bf16[4,320,128]{2,1,0:T(8,128)(2,1)} %get-tuple-element.7), calls=%async_computation | async-start | bytes 655360 | tf_op jit(solution)/shard_map/all_to_all | solution.py:330
  9.5 14.2 %collective-permute-start = (bf16[35,4096]{1,0:T(8,128)(2,1)}, bf16[35,4096]{1,0:T(8,128)(2,1)S(1)}, u32[]{:S(2)}, u32[]{:S(2)}) collective-permute-start(bf16[35,4096]{1,0:T(8,128)(2,1)} %get-tuple-element.8.own_ref), channel_id=1, source_target_pairs={{0,1},{1,2},{2,3},{3,4},{4,5},{5,6},{6,7},{7,8},{8,9},{9,10},{10,1... | collective-permute-start | bytes 860168 | tf_op jit(solution)/shard_map/ppermute | solution.py:331
  12.8 11.3 %collective-permute-start.1 = (bf16[35,4096]{1,0:T(8,128)(2,1)}, bf16[35,4096]{1,0:T(8,128)(2,1)S(1)}, u32[]{:S(2)}, u32[]{:S(2)}) collective-permute-start(bf16[35,4096]{1,0:T(8,128)(2,1)} %get-tuple-element.8.own_ref), channel_id=1, source_target_pairs={{1,0},{2,1},{3,2},{4,3},{5,4},{6,5},{7,6},{8,7},{9,8},{10,9},{11,1... | collective-permute-start | bytes 860168 | tf_op jit(solution)/shard_map/ppermute | solution.py:332
  19.4 4.7 %copy-start.6 = (bf16[35,4096]{1,0:T(8,128)(2,1)S(1)}, bf16[35,4096]{1,0:T(8,128)(2,1)}, u32[]{:S(2)}) copy-start(bf16[35,4096]{1,0:T(8,128)(2,1)} %get-tuple-element.8.own_ref) | copy-start | bytes 860164
  19.4 4.7 %copy-start.7 = (s32[16,16]{1,0:T(8,128)S(1)}, s32[16,16]{1,0:T(8,128)}, u32[]{:S(2)}) copy-start(s32[16,16]{1,0:T(8,128)} %list_ref.3) | copy-start | bytes 3076
  19.4 4.7 %copy-start.8 = (s32[16]{0:T(128)S(1)}, s32[16]{0:T(128)}, u32[]{:S(2)}) copy-start(s32[16]{0:T(128)} %count_ref.3) | copy-start | bytes 196
  19.4 19.9 %all-to-all-start.1 = ((bf16[4,1184,128]{2,1,0:T(8,128)(2,1)}), bf16[4,1184,128]{2,1,0:T(8,128)(2,1)S(1)}, u32[]{:S(2)}, u32[]{:S(2)}) async-start(bf16[4,1184,128]{2,1,0:T(8,128)(2,1)} %regroup.1.first_ref), calls=%async_computation.1 | async-start | bytes 2424832 | tf_op jit(solution)/shard_map/all_to_all | solution.py:342
  39.2 18.9 %copy-start.3 = (s32[16,16]{1,0:T(8,128)S(1)}, s32[16,16]{1,0:T(8,128)}, u32[]{:S(2)}) copy-start(s32[16,16]{1,0:T(8,128)} %list_ref.4) | copy-start | bytes 3076
  39.2 18.9 %copy-start.4 = (s32[16]{0:T(128)S(1)}, s32[16]{0:T(128)}, u32[]{:S(2)}) copy-start(s32[16]{0:T(128)} %count_ref.4) | copy-start | bytes 196
  39.9 30.2 %all-to-all-start.2 = ((bf16[32,16,128]{2,1,0:T(8,128)(2,1)}), bf16[32,16,128]{2,1,0:T(8,128)(2,1)S(1)}, u32[]{:S(2)}, u32[]{:S(2)}) async-start(bf16[32,16,128]{2,1,0:T(8,128)(2,1)} %coarse.1.first_ref), calls=%async_computation.2 | async-start | bytes 262144 | tf_op jit(solution)/shard_map/all_to_all | solution.py:373
  58.1 2.2 %copy-start = (bf16[16,16,64,64]{3,2,1,0:T(8,128)(2,1)S(1)}, bf16[16,16,64,64]{3,2,1,0:T(8,128)(2,1)}, u32[]{:S(2)}) copy-start(bf16[16,16,64,64]{3,2,1,0:T(8,128)(2,1)} %coupling_ref.1) | copy-start | bytes 6291460
  60.3 9.8 %copy-start.1 = (bf16[16,64,256]{2,1,0:T(8,128)(2,1)S(1)}, bf16[16,64,256]{2,1,0:T(8,128)(2,1)}, u32[]{:S(2)}) copy-start(bf16[16,64,256]{2,1,0:T(8,128)(2,1)} %basis_ref.1) | copy-start | bytes 1572868
  60.3 9.8 %copy-start.2 = (bf16[16,64,64]{2,1,0:T(8,128)(2,1)S(1)}, bf16[16,64,64]{2,1,0:T(8,128)(2,1)}, u32[]{:S(2)}) copy-start(bf16[16,64,64]{2,1,0:T(8,128)(2,1)} %transfer_ref.1) | copy-start | bytes 393220
  60.3 9.8 %copy-start.5 = (s32[1,16]{1,0:T(1,128)S(1)}, s32[1,16]{1,0:T(1,128)}, u32[]{:S(2)}) copy-start(s32[1,16]{1,0:T(1,128)} %list_ref.5) | copy-start | bytes 196
